TPU v7x, 512 devices: a whole 4x8x8 slice. The times are simulated.
512 devices in a mesh: seq: 32 (over x, y), state: 16 (over z, core).
Axes of the slice: x: 4, y: 8, z: 8, core: 2. Of those that a mesh axis runs over, the one named last changes fastest.
Arguments:
- inputs: bfloat16 [16384, 2048], P('seq', 'state'), may hold values from -6 to 6
- out_grad: bfloat16 [16384, 2048], P('seq', 'state'), may hold values from -6 to 6
- in_proj: bfloat16 [2048, 2048], P('state'), may hold values from -0.125 to 0.125
- out_proj: bfloat16 [2048, 2048], P(None, 'state'), may hold values from -0.125 to 0.125
- rates: float32 [2048], P('state'), may hold values from 1.2207031e-05 to 0.03
- time_step: float32 [16384], P('seq'), may hold values from 0.5 to 65536, as said below
Outputs:
- grad_inputs: bfloat16 [16384, 2048], P('seq', 'state')
- grad_in_proj: float32 [2048, 2048], P('state')
- grad_out_proj: float32 [2048, 2048], P(None, 'state')
- grad_rates: float32 [2048], P('state')
Inputs may be any that keep to these rules, and one draw needn't show every extreme that they name: `time_step`: positive time steps.
All inputs are finite; a program needn't handle non-finite values.
Results may differ from a plain program's by a relative error of at most 0.017.
Values may be sent and summed in bfloat16 or wider, within the bound.
No kernel may reach another device: no remote copies, remote signals or barrier semaphores. Data moves between devices by JAX's collectives and lax.ppermute only.
A program may use at most 64 MiB of HBM per device.

v0:
```python
import jax
import jax.numpy as jnp
from jax import lax
from jax.sharding import PartitionSpec as P


def sent_together(arrays, axis, dim, along):
    widths = [a.shape[along] for a in arrays]
    both = jnp.concatenate(arrays, axis=along)
    filled = lax.all_gather(both, axis, axis=dim, tiled=True)
    return tuple(jnp.split(filled, [sum(widths[:k]) for k in range(1, len(widths))], axis=along))


def from_everyone(x, axis):
    copies = jnp.broadcast_to(x, (lax.axis_size(axis), *x.shape))
    return lax.all_to_all(copies, axis, split_axis=0, concat_axis=0, tiled=True)


def all_in_one(x, axis):
    leaves = jax.tree.leaves(x)
    order = sorted(range(len(leaves)), key=lambda k: -leaves[k].size)
    width = (1, *leaves[order[0]].shape)[-1]
    lines = [
        jnp.pad(leaves[k].reshape(-1), (0, -leaves[k].size % width)).reshape(-1, width)
        for k in order
    ]
    both, at, found = (from_everyone(jnp.concatenate(lines), axis), 0, {})
    for k, line in zip(order, lines):
        slab = both[:, at : at + len(line)].reshape(len(both), -1)
        found[k] = slab[:, : leaves[k].size].reshape(-1, *leaves[k].shape)
        at += len(line)
    numbers = iter(range(len(leaves)))
    return jax.tree.map(lambda _: found[next(numbers)], x)


def combined_pairwise(pieces, combine):
    while len(jax.tree.leaves(pieces)[0]) > 1:
        pieces = jax.vmap(combine)(
            *(jax.tree.map(lambda part: part[side::2], pieces) for side in (0, 1))
        )
    return jax.tree.map(lambda part: part[0], pieces)


def prefix(x, axis, combine, identity, reverse):
    devices, here = (lax.axis_size(axis), lax.axis_index(axis))
    passed = jnp.arange(devices) > here if reverse else jnp.arange(devices) < here

    def kept(part, zero, own):
        part = jnp.where(
            passed.reshape(-1, *(1 for _ in own.shape)), part, jnp.asarray(zero, own.dtype)
        )
        return part[::-1] if reverse else part

    pieces = all_in_one(x, axis)
    return combined_pairwise(jax.tree.map(kept, pieces, identity, x), combine)


def split_up(x, dim, devices):
    lengths = x.shape
    blocks = x.reshape(*lengths[:dim], devices, lengths[dim] // devices, *lengths[dim + 1 :])
    return jnp.moveaxis(blocks, dim, 0)


def summed_on_arrival(x, axis, dim):
    devices = lax.axis_size(axis)
    blocks = lax.all_to_all(split_up(x, dim, devices), axis, 0, 0, tiled=True)
    return jnp.sum(blocks.astype(jnp.float32), axis=0)


def combine(earlier, later):
    return (earlier[0] * later[0], later[0] * earlier[1] + later[1])


def on_device(inputs, out_grad, in_proj, out_proj, rates, time_step):
    gathered_inputs, complete_sensitivity = sent_together((inputs, out_grad), "state", 1, 0)
    decay = jnp.exp(-time_step[:, None] * rates[None, :])
    drive = lax.dot_general(
        gathered_inputs, in_proj, (((1,), (1,)), ((), ())), preferred_element_type=jnp.float32
    )
    adjoint_in = jnp.dot(complete_sensitivity, out_proj, preferred_element_type=jnp.float32)
    multiplied_terms, shard_states = lax.associative_scan(combine, (decay, drive), axis=0)
    coefs = jnp.concatenate([decay[1:], jnp.ones((1, decay.shape[1]), jnp.float32)], axis=0)
    back_products, back_local = lax.associative_scan(
        combine, (coefs[::-1], adjoint_in[::-1]), axis=0
    )
    remaining = back_products[::-1]
    adjoint_local = back_local[::-1]
    block_decay = multiplied_terms[-1]
    state_last = shard_states[-1]
    adjoint_first = decay[0] * adjoint_local[0]
    zeros_row = jnp.zeros_like(block_decay)
    ones_row = jnp.ones_like(block_decay)
    incoming_hidden = prefix(
        (block_decay, state_last), "seq", combine, (ones_row, zeros_row), False
    )[1]
    adjoint_carry = prefix(
        (block_decay, adjoint_first), "seq", combine, (ones_row, zeros_row), True
    )[1]
    states = shard_states + multiplied_terms * incoming_hidden[None, :]
    states_half = states.astype(jnp.bfloat16)
    output_gradient_piece = lax.dot_general(
        complete_sensitivity,
        states_half,
        (((0,), (0,)), ((), ())),
        preferred_element_type=jnp.float32,
    )
    adjoint = adjoint_local + remaining * adjoint_carry[None, :]
    adjoint_half = adjoint.astype(jnp.bfloat16)
    before = jnp.concatenate([incoming_hidden[None, :], states[:-1]], axis=0)
    rate_part = -jnp.sum(time_step[:, None] * decay * adjoint * before, axis=0)
    grad_in_part = lax.dot_general(
        adjoint_half, gathered_inputs, (((0,), (0,)), ((), ())), preferred_element_type=jnp.float32
    )
    input_terms = jnp.dot(adjoint_half, in_proj, preferred_element_type=jnp.float32)
    grad_inputs = summed_on_arrival(input_terms.astype(jnp.bfloat16), "state", 1).astype(
        jnp.bfloat16
    )
    grad_in_proj, grad_out_proj, grad_rates = lax.psum(
        (grad_in_part, output_gradient_piece, rate_part), "seq"
    )
    return (grad_inputs, grad_in_proj, grad_out_proj, grad_rates)


def solution(mesh):
    placed = (
        P("seq", "state"),
        P("seq", "state"),
        P("state", None),
        P(None, "state"),
        P("state"),
        P("seq"),
    )
    return jax.shard_map(
        on_device,
        mesh=mesh,
        in_specs=placed,
        out_specs=(P("seq", "state"), P("state", None), P(None, "state"), P("state")),
        check_vma=False,
    )
```

profile of v0, /device:TPU:64, one launch (start us, length us, event | category | flops | bytes accessed | tf_op | source)
XLA Modules:
  0.0 296.8 jit_solution(14229288472016533186)
XLA Ops:
  7.2 1.7 pad_maximum_fusion
  9.0 0.7 neg.7
  9.7 0.8 multiply_exponential_fusion
  10.5 0.3 slice.830
  10.8 0.1 slice.791
  11.4 0.2 slice.702
  11.7 54.9 %all-gather.2.cloned.1.call-done = bf16[1024,2048]{1,0:T(8,128)(2,1)} async-done(((bf16[1024,128]{1,0:T(8,128)(2,1)}), bf16[1024,2048]{1,0:T(8,128)(2,1)}) %all-gather.2.cloned.1.call-update) | async-done | bytes 4194320 | tf_op jit(solution)/shard_map/all_gather | solution.py:10
  66.7 2.3 fusion
  69.0 0.3 slice.899
  69.4 0.1 slice.859
  70.5 2.4 fusion.6
  75.4 0.3 slice-done
  75.8 0.2 slice.772
  77.2 0.6 broadcast_in_dim.45
  77.9 9.5 %all-to-all-start.2 = ((f32[32,2,128]{2,1,0:T(2,128)}), f32[32,2,128]{2,1,0:T(2,128)S(1)}, u32[]{:S(2)}, u32[]{:S(2)}) async-start(f32[32,2,128]{2,1,0:T(2,128)} %broadcast_in_dim.45), calls=%async_computation.2 | async-start | bytes 65536 | tf_op jit(solution)/shard_map/all_to_all | solution.py:16
  87.5 0.1 rev.4
  87.8 0.1 rev.5
  87.9 9.4 %all-to-all-done.2 = f32[32,2,128]{2,1,0:T(2,128)S(1)} async-done(((f32[32,2,128]{2,1,0:T(2,128)}), f32[32,2,128]{2,1,0:T(2,128)S(1)}, u32[]{:S(2)}, u32[]{:S(2)}) %all-to-all-start.2) | async-done | bytes 32800 | tf_op jit(solution)/shard_map/all_to_all | solution.py:16
  97.3 0.6 broadcast_in_dim.41
  97.9 3.9 %all-to-all-start = ((f32[32,2,128]{2,1,0:T(2,128)}), f32[32,2,128]{2,1,0:T(2,128)S(1)}, u32[]{:S(2)}, u32[]{:S(2)}) async-start(f32[32,2,128]{2,1,0:T(2,128)} %broadcast_in_dim.41), calls=%async_computation | async-start | bytes 65536 | tf_op jit(solution)/shard_map/all_to_all | solution.py:16
  102.2 9.4 %all-to-all-done = f32[32,2,128]{2,1,0:T(2,128)S(1)} async-done(((f32[32,2,128]{2,1,0:T(2,128)}), f32[32,2,128]{2,1,0:T(2,128)S(1)}, u32[]{:S(2)}, u32[]{:S(2)}) %all-to-all-start) | async-done | bytes 32800 | tf_op jit(solution)/shard_map/all_to_all | solution.py:16
  112.2 0.2 fusion.9
  112.4 0.7 fusion.8
  113.1 1.9 copy.21
  115.0 5.2 %all-to-all-start.1 = ((bf16[16,512,128]{2,1,0:T(8,128)(2,1)}), bf16[16,512,128]{2,1,0:T(8,128)(2,1)S(1)}, u32[]{:S(2)}, u32[]{:S(2)}) async-start(bf16[16,512,128]{2,1,0:T(8,128)(2,1)} %bitcast.29), calls=%async_computation.1 | async-start | bytes 4194304 | tf_op jit(solution)/shard_map/all_to_all | solution.py:66
  120.3 3.0 %fusion.2 = f32[128,2048]{1,0:T(8,128)} fusion(bf16[512,128]{1,0:T(8,128)(2,1)S(1)} %get-tuple-element.7, bf16[1024,2048]{1,0:T(8,128)(2,1)} %all-gather.2.cloned.1.call-done), kind=kOutput, calls=%fused_computation.4 | convolution fusion | flops 268435456 | bytes 3276800 | tf_op jit(solution)/shard_map/dot_general | solution.py:111
  123.3 3.3 %fusion.4 = f32[2048,128]{1,0:T(8,128)} fusion(bf16[1024,2048]{1,0:T(8,128)(2,1)} %all-gather.2.cloned.1.call-done, f32[512,128]{1,0:T(8,128)S(1)} %multiply_add_fusion), kind=kOutput, calls=%fused_computation.6 | convolution fusion | flops 268500992 | bytes 3407872 | tf_op jit(solution)/shard_map/dot_general | solution.py:101
  126.7 71.5 %psum.23 = f32[128]{0:T(128)} all-reduce(f32[128]{0:T(128)S(1)} %neg.8), channel_id=1, replica_groups=mesh['seq'=32,'state'=16] {'seq'}, use_global_device_ids=true, to_apply=%region_4.5 | all-reduce | flops 128 | bytes 1024 | tf_op jit(solution)/shard_map/psum | solution.py:118
  198.2 1.0 reduce_sum.21
  199.1 87.5 %all-reduce.77.cloned.1.call-done = (f32[128,2048]{1,0:T(8,128)}, f32[2048,128]{1,0:T(8,128)}) async-done(((f32[128,2048]{1,0:T(8,128)}, f32[2048,128]{1,0:T(8,128)}), (f32[128,2048]{1,0:T(8,128)}, f32[2048,128]{1,0:T(8,128)})) %all-reduce.77.cloned.1.call-update) | async-done | bytes 2097168 | tf_op jit(solution)/shard_map/psum | solution.py:118
  286.6 2.4 copy.24
  289.0 1.0 copy.25
  (354 shorter events, 5.2 us)
Async XLA Ops:
  7.2 59.5 %copy-start = (bf16[128,2048]{1,0:T(8,128)(2,1)S(1)}, bf16[128,2048]{1,0:T(8,128)(2,1)}, u32[]{:S(2)}) copy-start(bf16[128,2048]{1,0:T(8,128)(2,1)} %param.8) | copy-start | bytes 1572868
  7.2 59.5 %all-gather.2.cloned.1.call-start = ((), (), s32[]{:S(2)}) async-start(), calls=%async_computation.3 | async-start | bytes 4456448 | tf_op jit(solution)/shard_map/all_gather | solution.py:10
  69.0 3.9 %copy-start.2 = (f32[512,128]{1,0:T(8,128)}, f32[512,128]{1,0:T(8,128)S(1)}, u32[]{:S(2)}) copy-start(f32[512,128]{1,0:T(8,128)S(1)} %fusion) | copy-start | bytes 786436
  75.0 0.7 slice-start
  77.9 19.4 %all-to-all-start.2 = ((f32[32,2,128]{2,1,0:T(2,128)}), f32[32,2,128]{2,1,0:T(2,128)S(1)}, u32[]{:S(2)}, u32[]{:S(2)}) async-start(f32[32,2,128]{2,1,0:T(2,128)} %broadcast_in_dim.45), calls=%async_computation.2 | async-start | bytes 65536 | tf_op jit(solution)/shard_map/all_to_all | solution.py:16
  87.6 24.5 %copy-start.3 = (f32[512]{0:T(512)S(1)}, f32[512]{0:T(512)}, u32[]{:S(2)}) copy-start(f32[512]{0:T(512)} %param.11) | copy-start | bytes 6148
  87.7 24.5 %copy-start.4 = (f32[128]{0:T(128)S(1)}, f32[128]{0:T(128)}, u32[]{:S(2)}) copy-start(f32[128]{0:T(128)} %param.10) | copy-start | bytes 1540
  97.9 13.7 %all-to-all-start = ((f32[32,2,128]{2,1,0:T(2,128)}), f32[32,2,128]{2,1,0:T(2,128)S(1)}, u32[]{:S(2)}, u32[]{:S(2)}) async-start(f32[32,2,128]{2,1,0:T(2,128)} %broadcast_in_dim.41), calls=%async_computation | async-start | bytes 65536 | tf_op jit(solution)/shard_map/all_to_all | solution.py:16
  115.0 83.1 %all-to-all-start.1 = ((bf16[16,512,128]{2,1,0:T(8,128)(2,1)}), bf16[16,512,128]{2,1,0:T(8,128)(2,1)S(1)}, u32[]{:S(2)}, u32[]{:S(2)}) async-start(bf16[16,512,128]{2,1,0:T(8,128)(2,1)} %bitcast.29), calls=%async_computation.1 | async-start | bytes 4194304 | tf_op jit(solution)/shard_map/all_to_all | solution.py:66
  120.2 166.4 %all-reduce.77.cloned.1.call-start = ((), (), s32[]{:S(2)}) async-start(), calls=%async_computation.4 | async-start | bytes 4194304 | tf_op jit(solution)/shard_map/psum | solution.py:118
  286.6 2.4 copy-start.1
Sparse Core Ops, SparseCore 0:
  10.6 55.9 all-gather.1
  126.8 159.7 all-reduce.76
where the time goes:
time: 297 us
  waiting for transfers between devices  161 us (54%)
  blocking collectives  71.5 us (24%)
  starting transfers between devices  18.7 us (6%)
  between operations  15.9 us (5%)
  local copies, waits for them, and re-layouts  11.9 us (4%)
  matrix products  11.7 us (4%)
  other arithmetic  5.77 us (2%)
    psum x1, waiting for transfers between devices, on_device(): lax.psum((grad_in_part, output_gradient_piece, rate_part), 'seq')  87.5 us
    psum x1, blocking collectives, on_device(): lax.psum((grad_in_part, output_gradient_piece, rate_part), 'seq')  71.5 us
    all_gather x1, waiting for transfers between devices, sent_together(): filled = lax.all_gather(both, axis, axis=dim, tiled=True)  54.9 us
    all_to_all x2, waiting for transfers between devices, from_everyone(): return lax.all_to_all(copies, axis, split_axis=0, concat_axis=0, tiled=True)  18.8 us
    all_to_all x2, starting transfers between devices, from_everyone(): return lax.all_to_all(copies, axis, split_axis=0, concat_axis=0, tiled=True)  13.4 us
  transfers between devices with their start and end apart: 5, of which 4 were waited for; matrix products, arithmetic and copies ran while one was open for 4% of the time, Pallas kernels for 0%

commit v1 on v0

v1 whole, which is shorter than its diff:
```python
import jax
import jax.numpy as jnp
from jax import lax
from jax.experimental import pallas as pl
from jax.experimental.pallas import tpu as pltpu
from jax.sharding import PartitionSpec as P

F32 = jnp.float32
BF16 = jnp.bfloat16
LANES = 128
ROWS = 8
LIMIT = 48 * 1024 * 1024


def call(kernel, out_shape, scratch=(), cost=None, **specs):
    return pl.pallas_call(
        kernel,
        out_shape=out_shape,
        **specs,
        scratch_shapes=list(scratch),
        compiler_params=pltpu.CompilerParams(vmem_limit_bytes=LIMIT),
        cost_estimate=cost,
    )


def estimate(flops, nbytes):
    return pl.CostEstimate(flops=flops, bytes_accessed=nbytes, transcendentals=0)


def strand(step, tokens):
    return pl.ds(step, ROWS, tokens // ROWS)


def by_rows(values, last_first):
    rows, total = [None] * ROWS, jnp.ones_like(values[0:1])
    for k in reversed(range(ROWS)) if last_first else range(ROWS):
        rows[k] = total
        total = total * values[k : k + 1]
    return jnp.concatenate(rows, axis=0), total


def decays_kernel(
    dt_ref, rates_ref, dec_ref, cum_ref, rem_ref, out_cum, out_rem, w_ad, w_a, w_b, bd_ref
):
    tokens = dt_ref.shape[0]
    steps = tokens // ROWS
    dec_ref[...] = jnp.exp(-dt_ref[...] * rates_ref[...])
    total = dec_ref[strand(0, tokens), :]
    cum_ref[strand(0, tokens), :] = total
    for j in range(1, steps):
        total = total * dec_ref[strand(j, tokens), :]
        cum_ref[strand(j, tokens), :] = total
    ahead = jnp.ones_like(total)
    for j in reversed(range(steps)):
        rem_ref[strand(j, tokens), :] = ahead
        ahead = ahead * dec_ref[strand(j, tokens), :]
    before, whole = by_rows(total, False)
    after, _ = by_rows(total, True)
    for j in range(steps):
        at = strand(j, tokens)
        out_cum[at, :] = cum_ref[at, :] * before
        out_rem[at, :] = rem_ref[at, :] * after
    w_ad[...] = dt_ref[...] * dec_ref[...]
    w_a[...] = dt_ref[...] * out_cum[...]
    w_b[...] = w_ad[...] * out_rem[...]
    bd_ref[0:1, :] = whole
    bd_ref[1:2, :] = whole * jnp.sum(jnp.broadcast_to(dt_ref[...], dec_ref.shape), axis=0, keepdims=True)


def scans_kernel(
    g_ref, inp_ref, outp_ref, dec_ref, cum_ref, rem_ref, w_ad, w_a, w_b, bd_ref,
    st_ref, ad_ref, carry_ref, drive, adj_in,
):
    blocks, both, _ = g_ref.shape
    tokens = both // 2
    steps = tokens // ROWS
    x = jnp.concatenate([g_ref[k, :tokens, :] for k in range(blocks)], axis=1)
    drive[...] = lax.dot_general(x, inp_ref[...], (((1,), (1,)), ((), ())), preferred_element_type=F32)
    y = jnp.concatenate([g_ref[k, tokens:, :] for k in range(blocks)], axis=1)
    adj_in[...] = jnp.dot(y, outp_ref[...], preferred_element_type=F32)
    state = drive[strand(0, tokens), :]
    st_ref[strand(0, tokens), :] = state
    for j in range(1, steps):
        at = strand(j, tokens)
        state = dec_ref[at, :] * state + drive[at, :]
        st_ref[at, :] = state
    adjoint = adj_in[strand(steps - 1, tokens), :]
    ad_ref[strand(steps - 1, tokens), :] = adjoint
    for j in reversed(range(steps - 1)):
        at = strand(j, tokens)
        adjoint = dec_ref[strand(j + 1, tokens), :] * adjoint + adj_in[at, :]
        ad_ref[at, :] = adjoint
    span = cum_ref[strand(steps - 1, tokens), :]
    first = dec_ref[strand(0, tokens), :] * adjoint
    rows, entering = [], jnp.zeros((1, LANES), F32)
    for k in range(ROWS):
        rows.append(entering)
        entering = span[k : k + 1] * entering + state[k : k + 1]
    into = jnp.concatenate(rows, axis=0)
    rows, leaving = [None] * ROWS, jnp.zeros((1, LANES), F32)
    for k in reversed(range(ROWS)):
        rows[k] = leaving
        leaving = span[k : k + 1] * leaving + first[k : k + 1]
    back = jnp.concatenate(rows, axis=0)
    sums = [jnp.zeros((ROWS, LANES), F32)] * 3
    previous = into
    for j in range(steps):
        at = strand(j, tokens)
        state = st_ref[at, :] + cum_ref[at, :] * into
        adjoint = ad_ref[at, :] + rem_ref[at, :] * back
        st_ref[at, :] = state
        ad_ref[at, :] = adjoint
        sums = [
            sums[0] + w_ad[at, :] * adjoint * previous,
            sums[1] + w_a[at, :] * adjoint,
            sums[2] + w_b[at, :] * previous,
        ]
        previous = state
    sums = [jnp.sum(s, axis=0, keepdims=True) for s in sums]
    block = jnp.concatenate(
        [bd_ref[0:1, :], entering, leaving, *sums, bd_ref[1:2, :], jnp.zeros((1, LANES), F32)], axis=0
    )
    for s in range(carry_ref.shape[0]):
        carry_ref[s] = block


def products_kernel(
    me_ref, carry_ref, g_ref, st_ref, ad_ref, cum_ref, rem_ref,
    half_ref, grads_ref, rates_ref, into, back,
):
    devices = carry_ref.shape[0]
    blocks, both, _ = g_ref.shape
    tokens = both // 2
    entering = jnp.zeros((1, LANES), F32)
    for s in range(devices):
        into[s : s + 1, :] = entering
        entering = carry_ref[s, 0:1, :] * entering + carry_ref[s, 1:2, :]
    leaving = jnp.zeros((1, LANES), F32)
    total = jnp.zeros((1, LANES), F32)
    for s in reversed(range(devices)):
        back[s : s + 1, :] = leaving
        here = into[s : s + 1, :]
        total = total + (
            carry_ref[s, 3:4, :]
            + carry_ref[s, 4:5, :] * here
            + leaving * (carry_ref[s, 5:6, :] + carry_ref[s, 6:7, :] * here)
        )
        leaving = carry_ref[s, 0:1, :] * leaving + carry_ref[s, 2:3, :]
    rates_ref[...] = -total
    me = me_ref[0]
    adjoint = (ad_ref[...] + rem_ref[...] * back[pl.ds(me, 1), :]).astype(BF16)
    half_ref[...] = adjoint
    state = (st_ref[...] + cum_ref[...] * into[pl.ds(me, 1), :]).astype(BF16)
    half = LANES // 2
    pair = 2 * LANES
    for k in range(0, blocks, 2):
        x = jnp.concatenate([g_ref[k, :tokens, :], g_ref[k + 1, :tokens, :]], axis=1)
        y = jnp.concatenate([g_ref[k, tokens:, :], g_ref[k + 1, tokens:, :]], axis=1)
        gi = lax.dot_general(adjoint, x, (((0,), (0,)), ((), ())), preferred_element_type=F32)
        go = lax.dot_general(state, y, (((0,), (0,)), ((), ())), preferred_element_type=F32)
        for q in range(2):
            lanes = slice(q * LANES, (q + 1) * LANES)
            a = gi[:, lanes].astype(BF16)
            b = go[:, lanes].T.astype(BF16)
            for r in range(2):
                rows = slice(r * half, (r + 1) * half)
                grads_ref[2 * (k + q) + r, :half, :] = a[rows]
                grads_ref[2 * (k + q) + r, half:, :] = b[rows]


def sum_kernel(parts_ref, out_ref):
    total = parts_ref[0].astype(F32)
    for s in range(1, parts_ref.shape[0]):
        total = total + parts_ref[s].astype(F32)
    total = total.astype(BF16)
    for s in range(out_ref.shape[0]):
        out_ref[s] = total


def finish_kernel(parts_ref, gi_ref, go_ref):
    half = LANES // 2
    for k in range(parts_ref.shape[0] // 2):
        for r in range(2):
            rows = slice(r * half, (r + 1) * half)
            gi_ref[rows, k * LANES : (k + 1) * LANES] = parts_ref[2 * k + r, :half, :].astype(F32)
            go_ref[k * LANES + r * half : k * LANES + (r + 1) * half, :] = parts_ref[2 * k + r, half:, :].astype(F32)


def inputs_kernel(half_ref, col_ref, out_ref):
    blocks = half_ref.shape[0]
    a = jnp.concatenate([half_ref[k] for k in range(blocks)], axis=1)
    w = jnp.concatenate([col_ref[k] for k in range(blocks)], axis=0)
    out_ref[...] = jnp.dot(a, w, preferred_element_type=F32).astype(BF16)


def on_device(inputs, out_grad, in_proj, out_proj, rates, time_step):
    tokens = inputs.shape[0]
    features = in_proj.shape[1]
    blocks = lax.axis_size("state")
    devices = lax.axis_size("seq")
    sds = jax.ShapeDtypeStruct
    seen = sds((tokens, LANES), F32)
    gathered = lax.all_gather(jnp.concatenate([inputs, out_grad], axis=0), "state", axis=0)
    columns = lax.all_to_all(
        jnp.moveaxis(in_proj.reshape(LANES, blocks, LANES), 1, 0), "state", 0, 0, tiled=True
    )
    dec, near, far, cum, rem, *weights = call(
        decays_kernel,
        (seen,) * 8 + (sds((2, LANES), F32),),
    )(time_step[:, None], rates[None, :])
    states, adjoints, carry = call(
        scans_kernel,
        (seen, seen, sds((devices, ROWS, LANES), F32)),
        scratch=[pltpu.VMEM((tokens, LANES), F32)] * 2,
        cost=estimate(4 * tokens * features * LANES, 7 << 20),
    )(gathered, in_proj, out_proj, dec, near, far, *weights)
    carry = lax.all_to_all(carry, "seq", 0, 0, tiled=True)
    me = lax.axis_index("seq").astype(jnp.int32).reshape(1)
    vmem = pl.BlockSpec(memory_space=pltpu.VMEM)
    half, grads, grad_rates = call(
        products_kernel,
        (
            sds((tokens, LANES), BF16),
            sds((devices, features * 2 // devices, LANES), BF16),
            sds((1, LANES), F32),
        ),
        in_specs=[pl.BlockSpec(memory_space=pltpu.SMEM)] + [vmem] * 6,
        scratch=[pltpu.VMEM((devices, LANES), F32)] * 2,
        cost=estimate(4 * tokens * features * LANES, 7 << 20),
    )(me, carry, gathered, states, adjoints, cum, rem)
    half_all = lax.all_gather(half, "state", axis=0)
    grads = lax.all_to_all(grads, "seq", 0, 0, tiled=True)
    grads = call(sum_kernel, sds(grads.shape, BF16))(grads)
    grads = lax.all_to_all(grads, "seq", 0, 0, tiled=True)
    grad_inputs = call(
        inputs_kernel,
        sds((tokens, LANES), BF16),
        cost=estimate(2 * tokens * features * LANES, 3 << 20),
    )(half_all, columns)
    grad_in, grad_out = call(
        finish_kernel, (sds((LANES, features), F32), sds((features, LANES), F32))
    )(grads)
    return grad_inputs, grad_in, grad_out, grad_rates[0]


def solution(mesh):
    placed = (
        P("seq", "state"),
        P("seq", "state"),
        P("state", None),
        P(None, "state"),
        P("state"),
        P("seq"),
    )
    return jax.shard_map(
        on_device,
        mesh=mesh,
        in_specs=placed,
        out_specs=(P("seq", "state"), P("state", None), P(None, "state"), P("state")),
        check_vma=False,
    )
```

time: 297 us -> 192 us (0.65)
  the two profiles are of different devices: /device:TPU:64 before, /device:TPU:8 now
where the time goes in v1:
time: 192 us; the launch traced here: 191 us
  waiting for transfers between devices  128 us (67%)
  starting transfers between devices  25.6 us (13%)
  Pallas kernels  15.7 us (8%)
  between operations  14.1 us (7%)
  local copies, waits for them, and re-layouts  6.43 us (3%)
    all_to_all x2, waiting for transfers between devices, on_device(): grads = lax.all_to_all(grads, 'seq', 0, 0, tiled=True)  51.7 us
    all_gather x1, waiting for transfers between devices, on_device(): lax.all_gather(jnp.concatenate([inputs, out_grad], axis=0), 'state', axis=0)  49.2 us
    all_to_all x1, waiting for transfers between devices, on_device(): lax.all_to_all(jnp.moveaxis(in_proj.reshape(LANES, blocks, LANES), 1, 0),...  16.1 us
    all_to_all x2, starting transfers between devices, on_device(): grads = lax.all_to_all(grads, 'seq', 0, 0, tiled=True)  11.3 us
    all_to_all x1, waiting for transfers between devices, on_device(): carry = lax.all_to_all(carry, 'seq', 0, 0, tiled=True)  10.1 us
    all_to_all x1, starting transfers between devices, on_device(): carry = lax.all_to_all(carry, 'seq', 0, 0, tiled=True)  9.98 us
    pallas_call x1, Pallas kernels, on_device(): call(scans_kernel, (seen, seen, sds((devices, ROWS, LANES), F32)), scratc...  6.29 us
    unnamed x11, local copies, waits for them, and re-layouts  4.59 us
  transfers between devices with their start and end apart: 6, of which 5 were waited for; matrix products, arithmetic and copies ran while one was open for 1% of the time, Pallas kernels for 2%

profile of v1, /device:TPU:8, one launch (start us, length us, event | category | flops | bytes accessed | tf_op | source)
XLA Modules:
  0.0 191.4 jit_solution(18173329209324130819)
XLA Ops:
  7.2 0.0 all-gather.5.cloned.1.call-start
  7.2 1.7 pad_maximum_fusion
  8.9 0.0 all-gather.5.cloned.1.call-update
  8.9 0.8 copy.10.dt_ref
  9.8 0.0 copy-start.4
  9.8 0.6 copy-done.4
  10.4 1.4 shard_map.93
  11.8 49.2 %all-gather.5.cloned.1.call-done = bf16[16384,128]{1,0:T(8,128)(2,1)} async-done(((bf16[1024,128]{1,0:T(8,128)(2,1)}), bf16[16384,128]{1,0:T(8,128)(2,1)}) %all-gather.5.cloned.1.call-update) | async-done | bytes 4194320 | tf_op jit(solution)/shard_map/all_gather | solution.py:203
  61.0 0.0 copy-start
  61.0 1.0 copy-done
  62.0 1.0 copy-done.3
  63.1 6.3 %shard_map.94 = (f32[512,128]{1,0:T(8,128)S(1)}, f32[512,128]{1,0:T(8,128)S(1)}, f32[32,8,128]{2,1,0:T(8,128)}) custom-call(bf16[16,1024,128]{2,1,0:T(8,128)(2,1)} %bitcast.10, bf16[128,2048]{1,0:T(8,128)(2,1)S(1)} %copy-done, bf16[2048,128]{1,0:T(8,128)(2,1)S(1)} %copy-done.3, f32[512,128]{1,0:T(8,128)S(1)} %get-tuple-element.21.dec_ref, ...), custom_call_target="tpu_custom_call" | custom-call | flops 536870912 | bytes 7340032 | tf_op jit(solution)/shard_map/pallas_call | solution.py:211
  69.3 10.0 %all-to-all-start = ((f32[32,8,128]{2,1,0:T(8,128)}), f32[32,8,128]{2,1,0:T(8,128)S(1)}, u32[]{:S(2)}, u32[]{:S(2)}) async-start(f32[32,8,128]{2,1,0:T(8,128)} %get-tuple-element.28), calls=%async_computation | async-start | bytes 262144 | tf_op jit(solution)/shard_map/all_to_all | solution.py:217
  79.3 10.1 %all-to-all-done.carry_ref = f32[32,8,128]{2,1,0:T(8,128)S(1)} async-done(((f32[32,8,128]{2,1,0:T(8,128)}), f32[32,8,128]{2,1,0:T(8,128)S(1)}, u32[]{:S(2)}, u32[]{:S(2)}) %all-to-all-start) | async-done | bytes 131104 | tf_op jit(solution)/shard_map/all_to_all | solution.py:217
  89.5 4.0 %shard_map.95 = (bf16[512,128]{1,0:T(8,128)(2,1)}, bf16[32,128,128]{2,1,0:T(8,128)(2,1)}, f32[1,128]{1,0:T(1,128)}) custom-call(s32[1]{0:T(128)} %bitcast.me_ref, f32[32,8,128]{2,1,0:T(8,128)S(1)} %all-to-all-done.carry_ref, bf16[16,1024,128]{2,1,0:T(8,128)(2,1)} %bitcast.11, f32[512,128]{1,0:T(8,128)S(1)} %get-tuple-element.29.st_ref, ...), custom_call_target="tpu_custom_call" | custom-call | flops 536870912 | bytes 7340032 | tf_op jit(solution)/shard_map/pallas_call | solution.py:220
  93.5 4.4 %all-to-all-start.2 = ((bf16[32,128,128]{2,1,0:T(8,128)(2,1)}), bf16[32,128,128]{2,1,0:T(8,128)(2,1)S(1)}, u32[]{:S(2)}, u32[]{:S(2)}) async-start(bf16[32,128,128]{2,1,0:T(8,128)(2,1)} %get-tuple-element.34), calls=%async_computation.2 | async-start | bytes 2097152 | tf_op jit(solution)/shard_map/all_to_all | solution.py:232
  97.9 0.0 all-gather.7.cloned.1.call-start
  98.0 0.7 all-gather.7.cloned.1.call-update
  98.7 0.0 copy-done.1
  98.7 0.3 copy.11
  98.9 1.0 copy.12
  100.0 26.0 %all-to-all-done.2.parts_ref = bf16[32,128,128]{2,1,0:T(8,128)(2,1)S(1)} async-done(((bf16[32,128,128]{2,1,0:T(8,128)(2,1)}), bf16[32,128,128]{2,1,0:T(8,128)(2,1)S(1)}, u32[]{:S(2)}, u32[]{:S(2)}) %all-to-all-start.2) | async-done | bytes 1048608 | tf_op jit(solution)/shard_map/all_to_all | solution.py:232
  125.9 4.2 %all-to-all-start.1 = ((bf16[16,128,128]{2,1,0:T(8,128)(2,1)}), bf16[16,128,128]{2,1,0:T(8,128)(2,1)S(1)}, u32[]{:S(2)}, u32[]{:S(2)}) async-start(bf16[16,128,128]{2,1,0:T(8,128)(2,1)} %bitcast.6), calls=%async_computation.1 | async-start | bytes 1048576 | tf_op jit(solution)/shard_map/all_to_all | solution.py:204
  130.2 1.2 shard_map.97
  131.4 16.1 %all-to-all-done.1.col_ref = bf16[16,128,128]{2,1,0:T(8,128)(2,1)S(1)} async-done(((bf16[16,128,128]{2,1,0:T(8,128)(2,1)}), bf16[16,128,128]{2,1,0:T(8,128)(2,1)S(1)}, u32[]{:S(2)}, u32[]{:S(2)}) %all-to-all-start.1) | async-done | bytes 524320 | tf_op jit(solution)/shard_map/all_to_all | solution.py:204
  147.5 6.9 %all-to-all-start.3 = ((bf16[32,128,128]{2,1,0:T(8,128)(2,1)}), bf16[32,128,128]{2,1,0:T(8,128)(2,1)S(1)}, u32[]{:S(2)}, u32[]{:S(2)}) async-start(bf16[32,128,128]{2,1,0:T(8,128)(2,1)} %shard_map.97), calls=%async_computation.3 | async-start | bytes 2097152 | tf_op jit(solution)/shard_map/all_to_all | solution.py:234
  154.3 0.0 all-gather.7.cloned.1.call-done
  154.4 0.0 copy-start.2
  154.4 1.6 copy-done.2
  155.9 1.4 shard_map.96
  157.3 25.7 %all-to-all-done.3.parts_ref = bf16[32,128,128]{2,1,0:T(8,128)(2,1)S(1)} async-done(((bf16[32,128,128]{2,1,0:T(8,128)(2,1)}), bf16[32,128,128]{2,1,0:T(8,128)(2,1)S(1)}, u32[]{:S(2)}, u32[]{:S(2)}) %all-to-all-start.3) | async-done | bytes 1048608 | tf_op jit(solution)/shard_map/all_to_all | solution.py:234
  183.1 1.5 shard_map.98
  (2 shorter events, 0.0 us)
Async XLA Ops:
  7.2 53.8 %all-gather.5.cloned.1.call-start = ((), (), s32[]{:S(2)}) async-start(), calls=%async_computation.4 | async-start | bytes 4456448 | tf_op jit(solution)/shard_map/all_gather | solution.py:203
  9.8 0.7 copy-start.4
  61.0 1.0 copy-start
  62.0 1.0 copy-start.3
  69.3 29.3 %copy-start.1 = (bf16[128,2048]{1,0:T(8,128)(2,1)S(1)}, bf16[128,2048]{1,0:T(8,128)(2,1)}, u32[]{:S(2)}) copy-start(bf16[128,2048]{1,0:T(8,128)(2,1)} %inp_ref.1) | copy-start | bytes 1572868
  69.3 20.1 %all-to-all-start = ((f32[32,8,128]{2,1,0:T(8,128)}), f32[32,8,128]{2,1,0:T(8,128)S(1)}, u32[]{:S(2)}, u32[]{:S(2)}) async-start(f32[32,8,128]{2,1,0:T(8,128)} %get-tuple-element.28), calls=%async_computation | async-start | bytes 262144 | tf_op jit(solution)/shard_map/all_to_all | solution.py:217
  93.5 32.5 %all-to-all-start.2 = ((bf16[32,128,128]{2,1,0:T(8,128)(2,1)}), bf16[32,128,128]{2,1,0:T(8,128)(2,1)S(1)}, u32[]{:S(2)}, u32[]{:S(2)}) async-start(bf16[32,128,128]{2,1,0:T(8,128)(2,1)} %get-tuple-element.34), calls=%async_computation.2 | async-start | bytes 2097152 | tf_op jit(solution)/shard_map/all_to_all | solution.py:232
  97.9 56.4 %all-gather.7.cloned.1.call-start = ((), (), s32[]{:S(2)}) async-start(), calls=%async_computation.5 | async-start | bytes 2228224 | tf_op jit(solution)/shard_map/all_gather | solution.py:231
  125.9 21.5 %all-to-all-start.1 = ((bf16[16,128,128]{2,1,0:T(8,128)(2,1)}), bf16[16,128,128]{2,1,0:T(8,128)(2,1)S(1)}, u32[]{:S(2)}, u32[]{:S(2)}) async-start(bf16[16,128,128]{2,1,0:T(8,128)(2,1)} %bitcast.6), calls=%async_computation.1 | async-start | bytes 1048576 | tf_op jit(solution)/shard_map/all_to_all | solution.py:204
  147.5 35.6 %all-to-all-start.3 = ((bf16[32,128,128]{2,1,0:T(8,128)(2,1)}), bf16[32,128,128]{2,1,0:T(8,128)(2,1)S(1)}, u32[]{:S(2)}, u32[]{:S(2)}) async-start(bf16[32,128,128]{2,1,0:T(8,128)(2,1)} %shard_map.97), calls=%async_computation.3 | async-start | bytes 2097152 | tf_op jit(solution)/shard_map/all_to_all | solution.py:234
  154.4 1.6 copy-start.2
Sparse Core Ops, SparseCore 0:
  10.7 50.2 all-gather.4
  101.4 46.1 all-gather.6

commit v2 on v1

v2 whole, which is shorter than its diff:
```python
import jax
import jax.numpy as jnp
from jax import lax
from jax.experimental import pallas as pl
from jax.experimental.pallas import tpu as pltpu
from jax.sharding import PartitionSpec as P

F32 = jnp.float32
BF16 = jnp.bfloat16
LANES = 128
ROWS = 8
INNER = 8
LIMIT = 32 * 1024 * 1024
VMEM = pl.BlockSpec(memory_space=pltpu.VMEM)
SMEM = pl.BlockSpec(memory_space=pltpu.SMEM)
HBM = pl.BlockSpec(memory_space=pltpu.HBM)
SCANS = 48 * 1024 * 1024
PRODS = 48 * 1024 * 1024
FINISH = 48 * 1024 * 1024
ANY = pl.BlockSpec(memory_space=pl.ANY)
DECAY, NEAR, FAR, BOTH, FIRST, SECOND, CUM, REM, KINDS = range(9)


def call(kernel, out_shape, scratch=(), cost=None, limit=LIMIT, **specs):
    return pl.pallas_call(
        kernel,
        out_shape=out_shape,
        **specs,
        scratch_shapes=list(scratch),
        compiler_params=pltpu.CompilerParams(vmem_limit_bytes=limit),
        cost_estimate=cost,
    )


def estimate(flops, nbytes):
    return pl.CostEstimate(flops=flops, bytes_accessed=nbytes, transcendentals=0)


def strand(step, tokens):
    return pl.ds(step, ROWS, tokens // ROWS)


def by_rows(values, last_first):
    rows, total = [None] * ROWS, jnp.ones_like(values[0:1])
    for k in reversed(range(ROWS)) if last_first else range(ROWS):
        rows[k] = total
        total = total * values[k : k + 1]
    return jnp.concatenate(rows, axis=0), total


def fetch(source, which, held, sems):
    copies = [
        pltpu.make_async_copy(source.at[w], held.at[n], sems.at[n]) for n, w in enumerate(which)
    ]
    for copy in copies:
        copy.start()
    return copies


def decays_kernel(dt_ref, rates_ref, col_ref, d_ref, ends_ref):
    tokens = dt_ref.shape[0]
    steps = tokens // ROWS
    dec_ref, near_ref, far_ref = d_ref.at[DECAY], d_ref.at[NEAR], d_ref.at[FAR]
    cum_ref, rem_ref = d_ref.at[CUM], d_ref.at[REM]
    dec_ref[...] = jnp.exp(-dt_ref[...] * rates_ref[...])
    total = dec_ref[strand(0, tokens), :]
    near_ref[strand(0, tokens), :] = total
    for j in range(1, steps):
        total = total * dec_ref[strand(j, tokens), :]
        near_ref[strand(j, tokens), :] = total
    ahead = jnp.ones_like(total)
    for j in reversed(range(steps)):
        far_ref[strand(j, tokens), :] = ahead
        ahead = ahead * dec_ref[strand(j, tokens), :]
    before, whole = by_rows(total, False)
    after, _ = by_rows(total, True)
    for j in range(steps):
        at = strand(j, tokens)
        cum_ref[at, :] = near_ref[at, :] * before
        rem_ref[at, :] = far_ref[at, :] * after
    d_ref[BOTH] = dt_ref[...] * dec_ref[...]
    d_ref[FIRST] = dt_ref[...] * cum_ref[...]
    d_ref[SECOND] = dt_ref[...] * dec_ref[...] * rem_ref[...]
    ends_ref[:ROWS, :] = total
    summed = jnp.sum(jnp.broadcast_to(dt_ref[...], dec_ref.shape), axis=0, keepdims=True)
    ends_ref[ROWS:, :] = jnp.concatenate(
        [whole, whole * summed, jnp.zeros((ROWS - 2, LANES), F32)], axis=0
    )


PARTS = 4


def join_kernel(a_ref, b_ref, out_ref, held, sems):
    rows = a_ref.shape[0]
    stays = [pl.ds(n * rows, rows) for n in range(2)]
    comes = [
        pltpu.make_async_copy(ref, held.at[at], sems.at[n])
        for n, (ref, at) in enumerate(zip((a_ref, b_ref), stays))
    ]
    goes = [
        pltpu.make_async_copy(held.at[at], out_ref.at[at], sems.at[2 + n])
        for n, at in enumerate(stays)
    ]
    for copy in comes:
        copy.start()
    for come, go in zip(comes, goes):
        come.wait()
        go.start()
    for copy in goes:
        copy.wait()


def fetch_parts(g_ref, held, sems):
    step = g_ref.shape[0] // PARTS
    copies = [
        pltpu.make_async_copy(
            g_ref.at[pl.ds(c * step, step)], held.at[pl.ds(c * step, step)], sems.at[c]
        )
        for c in range(PARTS)
    ]
    for copy in copies:
        copy.start()
    return copies, step


def scans_kernel(
    me_ref, g_ref, in_ref, out_ref, d_ref, ends_ref,
    st_ref, ad_ref, carry_ref, drive, adj_in, held, sems, kept, kept_sems, inp_ref, outp_ref, w_sems,
):
    weights = [
        pltpu.make_async_copy(in_ref, inp_ref, w_sems.at[0]),
        pltpu.make_async_copy(out_ref, outp_ref, w_sems.at[1]),
    ]
    for copy in weights:
        copy.start()
    copies, step = fetch_parts(g_ref, held, sems)
    others = fetch(d_ref, (DECAY, NEAR, FAR, BOTH, FIRST, SECOND), kept, kept_sems)
    tokens = st_ref.shape[0]
    steps = tokens // ROWS
    for copy in weights:
        copy.wait()
    x, y = 0.0, 0.0
    for c, copy in enumerate(copies):
        copy.wait()
        slabs = range(c * step, (c + 1) * step)
        span = slice(c * step * LANES, (c + 1) * step * LANES)
        x = x + lax.dot_general(
            jnp.concatenate([held[k, :tokens, :] for k in slabs], axis=1),
            inp_ref[:, span],
            (((1,), (1,)), ((), ())),
            preferred_element_type=F32,
        )
        y = y + jnp.dot(
            jnp.concatenate([held[k, tokens:, :] for k in slabs], axis=1),
            outp_ref[span, :],
            preferred_element_type=F32,
        )
    drive[...] = x
    adj_in[...] = y
    for copy in others:
        copy.wait()
    dec_ref, near_ref, far_ref, w_ad, w_a, w_b = [kept.at[n] for n in range(6)]
    state = drive[strand(0, tokens), :]
    st_ref[strand(0, tokens), :] = state
    for j in range(1, steps):
        at = strand(j, tokens)
        state = dec_ref[at, :] * state + drive[at, :]
        st_ref[at, :] = state
    adjoint = adj_in[strand(steps - 1, tokens), :]
    ad_ref[strand(steps - 1, tokens), :] = adjoint
    for j in reversed(range(steps - 1)):
        at = strand(j, tokens)
        adjoint = dec_ref[strand(j + 1, tokens), :] * adjoint + adj_in[at, :]
        ad_ref[at, :] = adjoint
    first = dec_ref[strand(0, tokens), :] * adjoint
    rows, entering = [], jnp.zeros((1, LANES), F32)
    for k in range(ROWS):
        rows.append(entering)
        entering = ends_ref[k : k + 1, :] * entering + state[k : k + 1]
    into = jnp.concatenate(rows, axis=0)
    rows, leaving = [None] * ROWS, jnp.zeros((1, LANES), F32)
    for k in reversed(range(ROWS)):
        rows[k] = leaving
        leaving = ends_ref[k : k + 1, :] * leaving + first[k : k + 1]
    back = jnp.concatenate(rows, axis=0)
    sums = [jnp.zeros((ROWS, LANES), F32)] * 3
    previous = into
    for j in range(steps):
        at = strand(j, tokens)
        state = st_ref[at, :] + near_ref[at, :] * into
        adjoint = ad_ref[at, :] + far_ref[at, :] * back
        st_ref[at, :] = state
        ad_ref[at, :] = adjoint
        sums = [
            sums[0] + w_ad[at, :] * adjoint * previous,
            sums[1] + w_a[at, :] * adjoint,
            sums[2] + w_b[at, :] * previous,
        ]
        previous = state
    sums = [jnp.sum(s, axis=0, keepdims=True) for s in sums]
    block = jnp.concatenate(
        [
            ends_ref[ROWS : ROWS + 1, :],
            entering,
            leaving,
            *sums,
            ends_ref[ROWS + 1 : ROWS + 2, :],
            jnp.zeros((1, LANES), F32),
        ],
        axis=0,
    )
    for s in range(carry_ref.shape[0]):
        carry_ref[s] = block


def products_kernel(
    me_ref, carry_ref, g_ref, st_ref, ad_ref, d_ref,
    half_ref, to_ref, rates_ref, into, back, held, sems, kept, kept_sems, grads_ref, to_sems,
):
    others = fetch(d_ref, (CUM, REM), kept, kept_sems)
    copies, step = fetch_parts(g_ref, held, sems)
    devices = carry_ref.shape[0]
    blocks, both, _ = g_ref.shape
    tokens = both // 2
    entering = jnp.zeros((1, LANES), F32)
    for s in range(devices):
        into[s : s + 1, :] = entering
        entering = carry_ref[s, 0:1, :] * entering + carry_ref[s, 1:2, :]
    leaving = jnp.zeros((1, LANES), F32)
    total = jnp.zeros((1, LANES), F32)
    for s in reversed(range(devices)):
        back[s : s + 1, :] = leaving
        here = into[s : s + 1, :]
        total = total + (
            carry_ref[s, 3:4, :]
            + carry_ref[s, 4:5, :] * here
            + leaving * (carry_ref[s, 5:6, :] + carry_ref[s, 6:7, :] * here)
        )
        leaving = carry_ref[s, 0:1, :] * leaving + carry_ref[s, 2:3, :]
    rates_ref[...] = -total
    me = me_ref[0]
    for copy in others:
        copy.wait()
    adjoint = (ad_ref[...] + kept[1] * back[pl.ds(me, 1), :]).astype(BF16)
    state = (st_ref[...] + kept[0] * into[pl.ds(me, 1), :]).astype(BF16)
    half_ref[...] = adjoint
    half = LANES // 2
    sent = []
    for k in range(0, blocks, 2):
        if k % step == 0:
            copies[k // step].wait()
        x = jnp.concatenate([held[k, :tokens, :], held[k + 1, :tokens, :]], axis=1)
        y = jnp.concatenate([held[k, tokens:, :], held[k + 1, tokens:, :]], axis=1)
        gi = lax.dot_general(adjoint, x, (((0,), (0,)), ((), ())), preferred_element_type=F32)
        go = lax.dot_general(state, y, (((0,), (0,)), ((), ())), preferred_element_type=F32)
        for q in range(2):
            lanes = slice(q * LANES, (q + 1) * LANES)
            a = gi[:, lanes].astype(BF16)
            b = go[:, lanes].T.astype(BF16)
            for r in range(2):
                rows = slice(r * half, (r + 1) * half)
                grads_ref[2 * (k + q) + r, :half, :] = a[rows]
                grads_ref[2 * (k + q) + r, half:, :] = b[rows]
        if (k + 2) % step == 0:
            c = k // step
            chunk = pl.ds(2 * c * step, 2 * step)
            sent.append(
                pltpu.make_async_copy(grads_ref.at[chunk], to_ref.at[chunk], to_sems.at[c])
            )
            sent[-1].start()
    for copy in sent:
        copy.wait()


def sum_kernel(parts_ref, out_ref):
    total = parts_ref[0].astype(F32)
    for s in range(1, parts_ref.shape[0]):
        total = total + parts_ref[s].astype(F32)
    out_ref[...] = total.astype(BF16)


def sum_and_repeat_kernel(parts_ref, out_ref):
    total = parts_ref[0].astype(F32)
    for s in range(1, parts_ref.shape[0]):
        total = total + parts_ref[s].astype(F32)
    total = total.astype(BF16)
    for s in range(out_ref.shape[0]):
        out_ref[s] = total


def repeat_kernel(part_ref, out_ref):
    for s in range(out_ref.shape[0]):
        out_ref[s] = part_ref[...]


def finish_kernel(half_ref, col_ref, parts_ref, out_ref, gi_ref, go_ref, held, sems):
    copies, step = fetch_parts(half_ref, held, sems)
    half = LANES // 2
    for k in range(parts_ref.shape[0] // 2):
        for r in range(2):
            rows = slice(r * half, (r + 1) * half)
            gi_ref[rows, k * LANES : (k + 1) * LANES] = parts_ref[2 * k + r, :half, :].astype(F32)
            rows = slice(k * LANES + r * half, k * LANES + (r + 1) * half)
            go_ref[rows, :] = parts_ref[2 * k + r, half:, :].astype(F32)
    total = 0.0
    for c, copy in enumerate(copies):
        copy.wait()
        slabs = range(c * step, (c + 1) * step)
        a = jnp.concatenate([held[k] for k in slabs], axis=1)
        w = jnp.concatenate([col_ref[k] for k in slabs], axis=0)
        total = total + jnp.dot(a, w, preferred_element_type=F32)
    out_ref[...] = total.astype(BF16)


def on_device(inputs, out_grad, in_proj, out_proj, rates, time_step):
    tokens = inputs.shape[0]
    features = in_proj.shape[1]
    blocks = lax.axis_size("state")
    devices = lax.axis_size("seq")
    outer = devices // INNER
    along_y = [[x * INNER + y for y in range(INNER)] for x in range(outer)]
    along_x = [[x * INNER + y for x in range(outer)] for y in range(INNER)]
    sds = jax.ShapeDtypeStruct
    seen = sds((tokens, LANES), F32)
    me = lax.axis_index("seq").astype(jnp.int32).reshape(1)

    def exchange(x, groups):
        return lax.all_to_all(x, "seq", 0, 0, tiled=True, axis_index_groups=groups)

    def parted(shape):
        return [pltpu.VMEM(shape, BF16), pltpu.SemaphoreType.DMA((PARTS,))]

    def kept(number):
        return [pltpu.VMEM((number, tokens, LANES), F32), pltpu.SemaphoreType.DMA((number,))]

    together = call(
        join_kernel,
        sds((2 * tokens, LANES), BF16),
        in_specs=[HBM] * 2,
        out_specs=HBM,
        scratch=[pltpu.VMEM((2 * tokens, LANES), BF16), pltpu.SemaphoreType.DMA((4,))],
        limit=60 * 1024 * 1024,
    )(inputs, out_grad)
    gathered = lax.all_gather(together, "state", axis=0)
    columns = lax.all_to_all(
        jnp.moveaxis(in_proj.reshape(LANES, blocks, LANES), 1, 0), "state", 0, 0, tiled=True
    )
    decays, ends = call(
        decays_kernel,
        (sds((KINDS, tokens, LANES), F32), sds((2 * ROWS, LANES), F32)),
        in_specs=[VMEM] * 2 + [ANY],
    )(time_step[:, None], rates[None, :], columns)
    states, adjoints, carry = call(
        scans_kernel,
        (seen, seen, sds((devices, ROWS, LANES), F32)),
        in_specs=[SMEM] + [HBM] * 3 + [ANY, VMEM],
        scratch=[pltpu.VMEM((tokens, LANES), F32)] * 2
        + parted(gathered.shape)
        + kept(6)
        + [
            pltpu.VMEM(in_proj.shape, BF16),
            pltpu.VMEM(out_proj.shape, BF16),
            pltpu.SemaphoreType.DMA((2,)),
        ],
        cost=estimate(4 * tokens * features * LANES, 7 << 20),
        limit=SCANS,
    )(me, gathered, in_proj, out_proj, decays, ends)
    carry = exchange(carry, None)
    half, grads, grad_rates = call(
        products_kernel,
        (
            sds((tokens, LANES), BF16),
            sds((devices, features * 2 // devices, LANES), BF16),
            sds((1, LANES), F32),
        ),
        in_specs=[SMEM, VMEM, HBM, VMEM, VMEM, ANY],
        out_specs=[VMEM, HBM, VMEM],
        scratch=[pltpu.VMEM((devices, LANES), F32)] * 2
        + parted(gathered.shape)
        + kept(2)
        + parted((devices, features * 2 // devices, LANES)),
        cost=estimate(4 * tokens * features * LANES, 7 << 20),
        limit=PRODS,
    )(me, carry, gathered, states, adjoints, decays)
    half_all = lax.all_gather(half, "state", axis=0)
    rows = grads.shape[1]
    part = sds((INNER * rows, LANES), BF16)
    grads = exchange(grads.reshape(outer, INNER * rows, LANES), along_x)
    grads = call(sum_kernel, part)(grads)
    grads = exchange(grads.reshape(INNER, rows, LANES), along_y)
    grads = call(sum_and_repeat_kernel, sds((INNER, rows, LANES), BF16))(grads)
    grads = exchange(grads, along_y)
    grads = call(repeat_kernel, sds((outer, *part.shape), BF16))(grads.reshape(part.shape))
    grads = exchange(grads, along_x).reshape(devices, rows, LANES)
    grad_inputs, grad_in, grad_out = call(
        finish_kernel,
        (
            sds((tokens, LANES), BF16),
            sds((LANES, features), F32),
            sds((features, LANES), F32),
        ),
        in_specs=[HBM, VMEM, VMEM],
        scratch=parted(half_all.shape),
        limit=FINISH,
    )(half_all, columns, grads)
    return grad_inputs, grad_in, grad_out, grad_rates[0]


def solution(mesh):
    placed = (
        P("seq", "state"),
        P("seq", "state"),
        P("state", None),
        P(None, "state"),
        P("state"),
        P("seq"),
    )
    return jax.shard_map(
        on_device,
        mesh=mesh,
        in_specs=placed,
        out_specs=(P("seq", "state"), P("state", None), P(None, "state"), P("state")),
        check_vma=False,
    )
```

time: 192 us -> 165 us (0.86)
  the two profiles are of different devices: /device:TPU:8 before, /device:TPU:2 now
where the time goes in v2:
time: 165 us
  blocking collectives  77.8 us (47%)
  waiting for transfers between devices  41.1 us (25%)
  Pallas kernels  15.2 us (9%)
  between operations  14.2 us (9%)
  starting transfers between devices  10.5 us (6%)
  local copies, waits for them, and re-layouts  6.14 us (4%)
    all_to_all x5, blocking collectives, exchange(): return lax.all_to_all(x, 'seq', 0, 0, tiled=True, axis_index_groups=groups)  77.8 us
    all_gather x1, waiting for transfers between devices, on_device(): gathered = lax.all_gather(together, 'state', axis=0)  23.7 us
    all_to_all x1, waiting for transfers between devices, on_device(): lax.all_to_all(jnp.moveaxis(in_proj.reshape(LANES, blocks, LANES), 1, 0),...  17.3 us
    all_to_all x1, starting transfers between devices, on_device(): lax.all_to_all(jnp.moveaxis(in_proj.reshape(LANES, blocks, LANES), 1, 0),...  10.4 us
    pallas_call x1, Pallas kernels, on_device(): call(scans_kernel, (seen, seen, sds((devices, ROWS, LANES), F32)), in_spe...  5.37 us
    unnamed x13, local copies, waits for them, and re-layouts  4.99 us
    pallas_call x1, Pallas kernels, on_device(): call(products_kernel, (sds((tokens, LANES), BF16), sds((devices, features...  3.6 us
  transfers between devices with their start and end apart: 3, of which 2 were waited for; matrix products, arithmetic and copies ran while one was open for 2% of the time, Pallas kernels for 1%

profile of v2, /device:TPU:2, one launch (start us, length us, event | category | flops | bytes accessed | tf_op | source)
XLA Modules:
  0.0 164.9 jit_solution(4074550061742642944)
XLA Ops:
  7.2 0.0 copy-start.5
  7.2 0.0 copy-start.4
  7.2 0.0 all-gather.5.cloned.1.call-start
  7.2 1.7 %shard_map.93 = bf16[1024,128]{1,0:T(8,128)(2,1)} custom-call(bf16[512,128]{1,0:T(8,128)(2,1)} %a_ref.1, bf16[512,128]{1,0:T(8,128)(2,1)} %b_ref.1), custom_call_target="tpu_custom_call" | custom-call | tf_op jit(solution)/shard_map/pallas_call | solution.py:337
  8.9 0.0 all-gather.5.cloned.1.call-update
  8.9 0.0 copy-start.1
  8.9 1.4 copy.10
  10.3 1.0 copy.11
  11.3 10.4 %all-to-all-start = ((bf16[16,128,128]{2,1,0:T(8,128)(2,1)}), bf16[16,128,128]{2,1,0:T(8,128)(2,1)S(1)}, u32[]{:S(2)}, u32[]{:S(2)}) async-start(bf16[16,128,128]{2,1,0:T(8,128)(2,1)} %bitcast.5), calls=%async_computation | async-start | bytes 1048576 | tf_op jit(solution)/shard_map/all_to_all | solution.py:346
  21.8 0.0 all-gather.7.cloned.1.call-start
  21.8 0.0 copy-done.5
  21.8 0.1 copy.12.dt_ref
  22.0 17.3 %all-to-all-done.col_ref = bf16[16,128,128]{2,1,0:T(8,128)(2,1)S(1)} async-done(((bf16[16,128,128]{2,1,0:T(8,128)(2,1)}), bf16[16,128,128]{2,1,0:T(8,128)(2,1)S(1)}, u32[]{:S(2)}, u32[]{:S(2)}) %all-to-all-start) | async-done | bytes 524320 | tf_op jit(solution)/shard_map/all_to_all | solution.py:346
  39.3 0.0 copy-done.4
  39.3 1.4 shard_map.94
  40.7 23.7 %all-gather.5.cloned.1.call-done = bf16[16384,128]{1,0:T(8,128)(2,1)} async-done(((bf16[1024,128]{1,0:T(8,128)(2,1)}), bf16[16384,128]{1,0:T(8,128)(2,1)}) %all-gather.5.cloned.1.call-update) | async-done | bytes 4194320 | tf_op jit(solution)/shard_map/all_gather | solution.py:345
  64.5 0.0 copy-done.1
  64.5 1.0 copy-done.3
  65.5 5.4 %shard_map.95 = (f32[512,128]{1,0:T(8,128)S(1)}, f32[512,128]{1,0:T(8,128)S(1)}, f32[32,8,128]{2,1,0:T(8,128)S(1)}) custom-call(s32[1]{0:T(128)} %bitcast.me_ref, bf16[16,1024,128]{2,1,0:T(8,128)(2,1)} %bitcast.18, bf16[128,2048]{1,0:T(8,128)(2,1)S(1)} %copy-done.1, bf16[2048,128]{1,0:T(8,128)(2,1)S(1)} %copy-done.3, ...), custom_call_target="tpu_custom_call" | custom-call | flops 536870912 | bytes 7340032 | tf_op jit(solution)/shard_map/pallas_call | solution.py:354
  70.9 19.6 %all_to_all.30.carry_ref = f32[32,8,128]{2,1,0:T(8,128)S(1)} all-to-all(f32[32,8,128]{2,1,0:T(8,128)S(1)} %get-tuple-element.17), channel_id=1, replica_groups=mesh['seq'=32,'state'=16] {'seq'}, dimensions={0} | all-to-all | bytes 262144 | tf_op jit(solution)/shard_map/all_to_all | solution.py:329
  90.5 3.6 %shard_map.96 = (bf16[512,128]{1,0:T(8,128)(2,1)}, bf16[32,128,128]{2,1,0:T(8,128)(2,1)S(1)}, f32[1,128]{1,0:T(1,128)}) custom-call(s32[1]{0:T(128)} %bitcast.me_ref, f32[32,8,128]{2,1,0:T(8,128)S(1)} %all_to_all.30.carry_ref, bf16[16,1024,128]{2,1,0:T(8,128)(2,1)} %bitcast.19, f32[512,128]{1,0:T(8,128)S(1)} %get-tuple-element.18.st_ref, ...), custom_call_target="tpu_custom_call" | custom-call | flops 536870912 | bytes 7340032 | tf_op jit(solution)/shard_map/pallas_call | solution.py:370
  94.1 0.0 copy-start.2
  94.1 1.0 copy-done.2
  95.1 0.0 all-gather.7.cloned.1.call-update
  95.1 17.4 %all_to_all.31.parts_ref = bf16[4,1024,128]{2,1,0:T(8,128)(2,1)S(1)} all-to-all(bf16[4,1024,128]{2,1,0:T(8,128)(2,1)} %bitcast.16), channel_id=1, replica_groups={{0,128,256,384},{16,144,272,400},{32,160,288,416},{48,176,304,432},{64,..., dimensions={0} | all-to-all | bytes 2097152 | tf_op jit(solution)/shard_map/all_to_all | solution.py:329
  112.5 0.1 shard_map.97
  112.6 14.0 %all_to_all.32.parts_ref = bf16[8,128,128]{2,1,0:T(8,128)(2,1)S(1)} all-to-all(bf16[8,128,128]{2,1,0:T(8,128)(2,1)S(1)} %bitcast.14), channel_id=1, replica_groups={{0,16,32,48,64,80,96,112},{128,144,160,176,192,208,224,240},{256,272,28..., dimensions={0} | all-to-all | bytes 524288 | tf_op jit(solution)/shard_map/all_to_all | solution.py:329
  126.6 12.9 %all_to_all.33 = bf16[8,128,128]{2,1,0:T(8,128)(2,1)S(1)} all-to-all(bf16[8,128,128]{2,1,0:T(8,128)(2,1)S(1)} %shard_map.98), channel_id=1, replica_groups={{0,16,32,48,64,80,96,112},{128,144,160,176,192,208,224,240},{256,272,28..., dimensions={0} | all-to-all | bytes 524288 | tf_op jit(solution)/shard_map/all_to_all | solution.py:329
  139.5 0.1 shard_map.99
  139.7 13.9 %all_to_all.34 = bf16[4,1024,128]{2,1,0:T(8,128)(2,1)S(1)} all-to-all(bf16[4,1024,128]{2,1,0:T(8,128)(2,1)S(1)} %shard_map.99), channel_id=1, replica_groups={{0,128,256,384},{16,144,272,400},{32,160,288,416},{48,176,304,432},{64,..., dimensions={0} | all-to-all | bytes 2097152 | tf_op jit(solution)/shard_map/all_to_all | solution.py:329
  153.6 1.6 copy-done
  155.2 2.8 %shard_map.100 = (bf16[512,128]{1,0:T(8,128)(2,1)}, f32[128,2048]{1,0:T(8,128)}, f32[2048,128]{1,0:T(8,128)}) custom-call(bf16[16,512,128]{2,1,0:T(8,128)(2,1)S(1)} %bitcast.13, bf16[16,128,128]{2,1,0:T(8,128)(2,1)S(1)} %all-to-all-done.col_ref, bf16[32,128,128]{2,1,0:T(8,128)(2,1)S(1)} %bitcast.12), custom_call_target="tpu_custom_call" | custom-call | tf_op jit(solution)/shard_map/pallas_call | solution.py:396
  (4 shorter events, 0.0 us)
Async XLA Ops:
  7.2 14.6 %copy-start.5 = (f32[512]{0:T(512)S(1)}, f32[512]{0:T(512)}, u32[]{:S(2)}) copy-start(f32[512]{0:T(512)} %param.11) | copy-start | bytes 6148
  7.2 32.1 %copy-start.4 = (f32[128]{0:T(128)S(1)}, f32[128]{0:T(128)}, u32[]{:S(2)}) copy-start(f32[128]{0:T(128)} %param.10) | copy-start | bytes 1540
  7.2 57.3 %all-gather.5.cloned.1.call-start = ((), (), s32[]{:S(2)}) async-start(), calls=%async_computation.6 | async-start | bytes 4456448 | tf_op jit(solution)/shard_map/all_gather | solution.py:345
  8.9 55.5 %copy-start.1 = (bf16[128,2048]{1,0:T(8,128)(2,1)S(1)}, bf16[128,2048]{1,0:T(8,128)(2,1)}, u32[]{:S(2)}) copy-start(bf16[128,2048]{1,0:T(8,128)(2,1)} %in_ref.1) | copy-start | bytes 1572868
  11.3 27.9 %all-to-all-start = ((bf16[16,128,128]{2,1,0:T(8,128)(2,1)}), bf16[16,128,128]{2,1,0:T(8,128)(2,1)S(1)}, u32[]{:S(2)}, u32[]{:S(2)}) async-start(bf16[16,128,128]{2,1,0:T(8,128)(2,1)} %bitcast.5), calls=%async_computation | async-start | bytes 1048576 | tf_op jit(solution)/shard_map/all_to_all | solution.py:346
  21.8 131.9 %all-gather.7.cloned.1.call-start = ((), (), s32[]{:S(2)}) async-start(), calls=%async_computation.7 | async-start | bytes 2228224 | tf_op jit(solution)/shard_map/all_gather | solution.py:386
  64.5 1.0 copy-start.3
  94.1 1.0 copy-start.2
  153.6 1.6 copy-start
Sparse Core Ops, SparseCore 0:
  10.7 53.6 all-gather.4
  95.2 36.5 all-gather.6

commit v3 on v2

--- a/solution.py
+++ b/solution.py
@@ -16,9 +16,9 @@
 HBM = pl.BlockSpec(memory_space=pltpu.HBM)
 SCANS = 48 * 1024 * 1024
 PRODS = 48 * 1024 * 1024
-FINISH = 48 * 1024 * 1024
 ANY = pl.BlockSpec(memory_space=pl.ANY)
-DECAY, NEAR, FAR, BOTH, FIRST, SECOND, CUM, REM, KINDS = range(9)
+DECAY, NEAR, FAR, NEXT, FIRST, KINDS = range(6)
+CUM, REM = range(2)
 
 
 def call(kernel, out_shape, scratch=(), cost=None, limit=LIMIT, **specs):
@@ -48,20 +48,13 @@
     return jnp.concatenate(rows, axis=0), total
 
 
-def fetch(source, which, held, sems):
-    copies = [
-        pltpu.make_async_copy(source.at[w], held.at[n], sems.at[n]) for n, w in enumerate(which)
-    ]
-    for copy in copies:
-        copy.start()
-    return copies
-
-
-def decays_kernel(dt_ref, rates_ref, col_ref, d_ref, ends_ref):
+def decays_kernel(
+    dt_ref, next_ref, rates_ref, inp_ref, outp_ref, col_ref, d_ref, b_ref, ends_ref
+):
     tokens = dt_ref.shape[0]
     steps = tokens // ROWS
     dec_ref, near_ref, far_ref = d_ref.at[DECAY], d_ref.at[NEAR], d_ref.at[FAR]
-    cum_ref, rem_ref = d_ref.at[CUM], d_ref.at[REM]
+    cum_ref, rem_ref = b_ref.at[CUM], b_ref.at[REM]
     dec_ref[...] = jnp.exp(-dt_ref[...] * rates_ref[...])
     total = dec_ref[strand(0, tokens), :]
     near_ref[strand(0, tokens), :] = total
@@ -78,9 +71,8 @@
         at = strand(j, tokens)
         cum_ref[at, :] = near_ref[at, :] * before
         rem_ref[at, :] = far_ref[at, :] * after
-    d_ref[BOTH] = dt_ref[...] * dec_ref[...]
+    d_ref[NEXT] = jnp.broadcast_to(next_ref[...], dec_ref.shape)
     d_ref[FIRST] = dt_ref[...] * cum_ref[...]
-    d_ref[SECOND] = dt_ref[...] * dec_ref[...] * rem_ref[...]
     ends_ref[:ROWS, :] = total
     summed = jnp.sum(jnp.broadcast_to(dt_ref[...], dec_ref.shape), axis=0, keepdims=True)
     ends_ref[ROWS:, :] = jnp.concatenate(
@@ -125,21 +117,12 @@
 
 
 def scans_kernel(
-    me_ref, g_ref, in_ref, out_ref, d_ref, ends_ref,
-    st_ref, ad_ref, carry_ref, drive, adj_in, held, sems, kept, kept_sems, inp_ref, outp_ref, w_sems,
+    me_ref, g_ref, inp_ref, outp_ref, d_ref, b_ref, ends_ref,
+    st_ref, ad_ref, carry_ref, drive, adj_in, held, sems,
 ):
-    weights = [
-        pltpu.make_async_copy(in_ref, inp_ref, w_sems.at[0]),
-        pltpu.make_async_copy(out_ref, outp_ref, w_sems.at[1]),
-    ]
-    for copy in weights:
-        copy.start()
     copies, step = fetch_parts(g_ref, held, sems)
-    others = fetch(d_ref, (DECAY, NEAR, FAR, BOTH, FIRST, SECOND), kept, kept_sems)
     tokens = st_ref.shape[0]
     steps = tokens // ROWS
-    for copy in weights:
-        copy.wait()
     x, y = 0.0, 0.0
     for c, copy in enumerate(copies):
         copy.wait()
@@ -158,46 +141,45 @@
         )
     drive[...] = x
     adj_in[...] = y
-    for copy in others:
-        copy.wait()
-    dec_ref, near_ref, far_ref, w_ad, w_a, w_b = [kept.at[n] for n in range(6)]
+    dec_ref = d_ref.at[DECAY]
     state = drive[strand(0, tokens), :]
     st_ref[strand(0, tokens), :] = state
     for j in range(1, steps):
         at = strand(j, tokens)
         state = dec_ref[at, :] * state + drive[at, :]
         st_ref[at, :] = state
+    reaching = jnp.zeros((ROWS, LANES), F32)
+    ad_ref[strand(steps - 1, tokens), :] = reaching
     adjoint = adj_in[strand(steps - 1, tokens), :]
-    ad_ref[strand(steps - 1, tokens), :] = adjoint
     for j in reversed(range(steps - 1)):
         at = strand(j, tokens)
-        adjoint = dec_ref[strand(j + 1, tokens), :] * adjoint + adj_in[at, :]
-        ad_ref[at, :] = adjoint
+        reaching = dec_ref[strand(j + 1, tokens), :] * adjoint
+        ad_ref[at, :] = reaching
+        adjoint = reaching + adj_in[at, :]
     first = dec_ref[strand(0, tokens), :] * adjoint
-    rows, entering = [], jnp.zeros((1, LANES), F32)
+    into, entering = [], jnp.zeros((1, LANES), F32)
     for k in range(ROWS):
-        rows.append(entering)
+        into.append(entering)
         entering = ends_ref[k : k + 1, :] * entering + state[k : k + 1]
-    into = jnp.concatenate(rows, axis=0)
-    rows, leaving = [None] * ROWS, jnp.zeros((1, LANES), F32)
+    back, leaving = [None] * ROWS, jnp.zeros((1, LANES), F32)
     for k in reversed(range(ROWS)):
-        rows[k] = leaving
+        back[k] = leaving
         leaving = ends_ref[k : k + 1, :] * leaving + first[k : k + 1]
-    back = jnp.concatenate(rows, axis=0)
     sums = [jnp.zeros((ROWS, LANES), F32)] * 3
-    previous = into
-    for j in range(steps):
-        at = strand(j, tokens)
-        state = st_ref[at, :] + near_ref[at, :] * into
-        adjoint = ad_ref[at, :] + far_ref[at, :] * back
-        st_ref[at, :] = state
-        ad_ref[at, :] = adjoint
-        sums = [
-            sums[0] + w_ad[at, :] * adjoint * previous,
-            sums[1] + w_a[at, :] * adjoint,
-            sums[2] + w_b[at, :] * previous,
-        ]
-        previous = state
+    for k in range(ROWS):
+        for j in range(k * steps, (k + 1) * steps, ROWS):
+            at = slice(j, j + ROWS)
+            state = st_ref[at, :] + d_ref[NEAR, at, :] * into[k]
+            reaching = ad_ref[at, :] + d_ref[FAR, at, :] * back[k]
+            adjoint = adj_in[at, :] + reaching
+            st_ref[at, :] = state
+            ad_ref[at, :] = adjoint
+            timed = d_ref[NEXT, at, :] * state
+            sums = [
+                sums[0] + timed * reaching,
+                sums[1] + d_ref[FIRST, at, :] * adjoint,
+                sums[2] + timed * b_ref[REM, at, :],
+            ]
     sums = [jnp.sum(s, axis=0, keepdims=True) for s in sums]
     block = jnp.concatenate(
         [
@@ -215,10 +197,9 @@
 
 
 def products_kernel(
-    me_ref, carry_ref, g_ref, st_ref, ad_ref, d_ref,
-    half_ref, to_ref, rates_ref, into, back, held, sems, kept, kept_sems, grads_ref, to_sems,
+    me_ref, carry_ref, g_ref, st_ref, ad_ref, b_ref,
+    half_ref, grads_ref, rates_ref, into, back, held, sems,
 ):
-    others = fetch(d_ref, (CUM, REM), kept, kept_sems)
     copies, step = fetch_parts(g_ref, held, sems)
     devices = carry_ref.shape[0]
     blocks, both, _ = g_ref.shape
@@ -240,13 +221,10 @@
         leaving = carry_ref[s, 0:1, :] * leaving + carry_ref[s, 2:3, :]
     rates_ref[...] = -total
     me = me_ref[0]
-    for copy in others:
-        copy.wait()
-    adjoint = (ad_ref[...] + kept[1] * back[pl.ds(me, 1), :]).astype(BF16)
-    state = (st_ref[...] + kept[0] * into[pl.ds(me, 1), :]).astype(BF16)
+    adjoint = (ad_ref[...] + b_ref[REM] * back[pl.ds(me, 1), :]).astype(BF16)
+    state = (st_ref[...] + b_ref[CUM] * into[pl.ds(me, 1), :]).astype(BF16)
     half_ref[...] = adjoint
     half = LANES // 2
-    sent = []
     for k in range(0, blocks, 2):
         if k % step == 0:
             copies[k // step].wait()
@@ -262,15 +240,6 @@
                 rows = slice(r * half, (r + 1) * half)
                 grads_ref[2 * (k + q) + r, :half, :] = a[rows]
                 grads_ref[2 * (k + q) + r, half:, :] = b[rows]
-        if (k + 2) % step == 0:
-            c = k // step
-            chunk = pl.ds(2 * c * step, 2 * step)
-            sent.append(
-                pltpu.make_async_copy(grads_ref.at[chunk], to_ref.at[chunk], to_sems.at[c])
-            )
-            sent[-1].start()
-    for copy in sent:
-        copy.wait()
 
 
 def sum_kernel(parts_ref, out_ref):
@@ -294,8 +263,15 @@
         out_ref[s] = part_ref[...]
 
 
-def finish_kernel(half_ref, col_ref, parts_ref, out_ref, gi_ref, go_ref, held, sems):
-    copies, step = fetch_parts(half_ref, held, sems)
+def inputs_kernel(half_ref, col_ref, out_ref, done_ref):
+    done_ref[...] = jnp.zeros_like(done_ref)
+    blocks = half_ref.shape[0]
+    a = jnp.concatenate([half_ref[k] for k in range(blocks)], axis=1)
+    w = jnp.concatenate([col_ref[k] for k in range(blocks)], axis=0)
+    out_ref[...] = jnp.dot(a, w, preferred_element_type=F32).astype(BF16)
+
+
+def finish_kernel(parts_ref, done_ref, gi_ref, go_ref):
     half = LANES // 2
     for k in range(parts_ref.shape[0] // 2):
         for r in range(2):
@@ -303,14 +279,6 @@
             gi_ref[rows, k * LANES : (k + 1) * LANES] = parts_ref[2 * k + r, :half, :].astype(F32)
             rows = slice(k * LANES + r * half, k * LANES + (r + 1) * half)
             go_ref[rows, :] = parts_ref[2 * k + r, half:, :].astype(F32)
-    total = 0.0
-    for c, copy in enumerate(copies):
-        copy.wait()
-        slabs = range(c * step, (c + 1) * step)
-        a = jnp.concatenate([held[k] for k in slabs], axis=1)
-        w = jnp.concatenate([col_ref[k] for k in slabs], axis=0)
-        total = total + jnp.dot(a, w, preferred_element_type=F32)
-    out_ref[...] = total.astype(BF16)
 
 
 def on_device(inputs, out_grad, in_proj, out_proj, rates, time_step):
@@ -331,9 +299,6 @@
     def parted(shape):
         return [pltpu.VMEM(shape, BF16), pltpu.SemaphoreType.DMA((PARTS,))]
 
-    def kept(number):
-        return [pltpu.VMEM((number, tokens, LANES), F32), pltpu.SemaphoreType.DMA((number,))]
-
     together = call(
         join_kernel,
         sds((2 * tokens, LANES), BF16),
@@ -346,26 +311,25 @@
     columns = lax.all_to_all(
         jnp.moveaxis(in_proj.reshape(LANES, blocks, LANES), 1, 0), "state", 0, 0, tiled=True
     )
-    decays, ends = call(
+    following = jnp.concatenate([time_step[1:], jnp.zeros((1,), F32)])
+    decays, whole, ends = call(
         decays_kernel,
-        (sds((KINDS, tokens, LANES), F32), sds((2 * ROWS, LANES), F32)),
-        in_specs=[VMEM] * 2 + [ANY],
-    )(time_step[:, None], rates[None, :], columns)
+        (
+            sds((KINDS, tokens, LANES), F32),
+            sds((2, tokens, LANES), F32),
+            sds((2 * ROWS, LANES), F32),
+        ),
+        in_specs=[VMEM] * 5 + [ANY],
+    )(time_step[:, None], following[:, None], rates[None, :], in_proj, out_proj, columns)
     states, adjoints, carry = call(
         scans_kernel,
         (seen, seen, sds((devices, ROWS, LANES), F32)),
-        in_specs=[SMEM] + [HBM] * 3 + [ANY, VMEM],
+        in_specs=[SMEM, HBM] + [VMEM] * 5,
         scratch=[pltpu.VMEM((tokens, LANES), F32)] * 2
-        + parted(gathered.shape)
-        + kept(6)
-        + [
-            pltpu.VMEM(in_proj.shape, BF16),
-            pltpu.VMEM(out_proj.shape, BF16),
-            pltpu.SemaphoreType.DMA((2,)),
-        ],
+        + parted(gathered.shape),
         cost=estimate(4 * tokens * features * LANES, 7 << 20),
         limit=SCANS,
-    )(me, gathered, in_proj, out_proj, decays, ends)
+    )(me, gathered, in_proj, out_proj, decays, whole, ends)
     carry = exchange(carry, None)
     half, grads, grad_rates = call(
         products_kernel,
@@ -374,15 +338,11 @@
             sds((devices, features * 2 // devices, LANES), BF16),
             sds((1, LANES), F32),
         ),
-        in_specs=[SMEM, VMEM, HBM, VMEM, VMEM, ANY],
-        out_specs=[VMEM, HBM, VMEM],
-        scratch=[pltpu.VMEM((devices, LANES), F32)] * 2
-        + parted(gathered.shape)
-        + kept(2)
-        + parted((devices, features * 2 // devices, LANES)),
+        in_specs=[SMEM, VMEM, HBM, VMEM, VMEM, VMEM],
+        scratch=[pltpu.VMEM((devices, LANES), F32)] * 2 + parted(gathered.shape),
         cost=estimate(4 * tokens * features * LANES, 7 << 20),
         limit=PRODS,
-    )(me, carry, gathered, states, adjoints, decays)
+    )(me, carry, gathered, states, adjoints, whole)
     half_all = lax.all_gather(half, "state", axis=0)
     rows = grads.shape[1]
     part = sds((INNER * rows, LANES), BF16)
@@ -393,17 +353,16 @@
     grads = exchange(grads, along_y)
     grads = call(repeat_kernel, sds((outer, *part.shape), BF16))(grads.reshape(part.shape))
     grads = exchange(grads, along_x).reshape(devices, rows, LANES)
-    grad_inputs, grad_in, grad_out = call(
+    grad_inputs, done = call(
+        inputs_kernel,
+        (sds((tokens, LANES), BF16), sds((ROWS, LANES), F32)),
+        cost=estimate(2 * tokens * features * LANES, 3 << 20),
+    )(half_all, columns)
+    grad_in, grad_out = call(
         finish_kernel,
-        (
-            sds((tokens, LANES), BF16),
-            sds((LANES, features), F32),
-            sds((features, LANES), F32),
-        ),
-        in_specs=[HBM, VMEM, VMEM],
-        scratch=parted(half_all.shape),
-        limit=FINISH,
-    )(half_all, columns, grads)
+        (sds((LANES, features), F32), sds((features, LANES), F32)),
+        in_specs=[VMEM, ANY],
+    )(grads, done)
     return grad_inputs, grad_in, grad_out, grad_rates[0]
 
 

time: 165 us -> 159 us (0.964)
  blocking collectives: 77.8 us -> 62.8 us
  starting transfers between devices: 10.5 us -> 15.4 us
  waiting for transfers between devices: 41.1 us -> 44.5 us
    all_to_all x5 -> x4, blocking collectives: 77.8 us -> 62.8 us  [exchange(): return lax.all_to_all(x, 'seq', 0, 0, tiled=True, axis_index_groups=groups)]
    all_to_all x0 -> x1, waiting for transfers between devices: none -> 7.22 us  [exchange(): return lax.all_to_all(x, 'seq', 0, 0, tiled=True, axis_index_groups=groups)]
    all_to_all x0 -> x1, starting transfers between devices: none -> 4.94 us  [exchange(): return lax.all_to_all(x, 'seq', 0, 0, tiled=True, axis_index_groups=groups)]
    all_gather x1, waiting for transfers between devices: 23.7 us -> 21.7 us  [on_device(): gathered = lax.all_gather(together, 'state', axis=0)]
    all_to_all x1, waiting for transfers between devices: 17.3 us -> 15.6 us  [on_device(): lax.all_to_all(jnp.moveaxis(in_proj.reshape(LANES, blocks, LANES), 1, 0),...]
    unnamed x13 -> x15, local copies, waits for them, and re-layouts: 4.99 us -> 4.9 us
    pallas_call x2 -> x3, Pallas kernels: 4.25 us -> 4.24 us  [the longest x1 1.5 us: on_device(): call(finish_kernel, (sds((LANES, features), F32), sds((features, LANES),...]
  transfers between devices with their start and end apart: 3 -> 4, of which waited for: 2 -> 3; matrix products, arithmetic and copies ran while one was open for 2% -> 3% of each run, Pallas kernels for 1% -> 3%
where the time goes in v3:
time: 159 us
  blocking collectives  62.8 us (39%)
  waiting for transfers between devices  44.5 us (28%)
  starting transfers between devices  15.4 us (10%)
  Pallas kernels  14.1 us (9%)
  between operations  14.1 us (9%)
  local copies, waits for them, and re-layouts  7.74 us (5%)
    all_to_all x4, blocking collectives, exchange(): return lax.all_to_all(x, 'seq', 0, 0, tiled=True, axis_index_groups=groups)  62.8 us
    all_gather x1, waiting for transfers between devices, on_device(): gathered = lax.all_gather(together, 'state', axis=0)  21.7 us
    all_to_all x1, waiting for transfers between devices, on_device(): lax.all_to_all(jnp.moveaxis(in_proj.reshape(LANES, blocks, LANES), 1, 0),...  15.6 us
    all_to_all x1, starting transfers between devices, on_device(): lax.all_to_all(jnp.moveaxis(in_proj.reshape(LANES, blocks, LANES), 1, 0),...  10.4 us
    all_to_all x1, waiting for transfers between devices, exchange(): return lax.all_to_all(x, 'seq', 0, 0, tiled=True, axis_index_groups=groups)  7.22 us
    all_to_all x1, starting transfers between devices, exchange(): return lax.all_to_all(x, 'seq', 0, 0, tiled=True, axis_index_groups=groups)  4.94 us
    unnamed x15, local copies, waits for them, and re-layouts  4.9 us
    pallas_call x1, Pallas kernels, on_device(): call(scans_kernel, (seen, seen, sds((devices, ROWS, LANES), F32)), in_spe...  3.91 us
  transfers between devices with their start and end apart: 4, of which 3 were waited for; matrix products, arithmetic and copies ran while one was open for 3% of the time, Pallas kernels for 3%

profile of v3, /device:TPU:2, one launch (start us, length us, event | category | flops | bytes accessed | tf_op | source)
XLA Modules:
  0.0 158.9 jit_solution(16800692923943561835)
XLA Ops:
  7.2 0.0 all-gather.5.cloned.1.call-start
  7.2 1.7 %shard_map.93 = bf16[1024,128]{1,0:T(8,128)(2,1)} custom-call(bf16[512,128]{1,0:T(8,128)(2,1)} %a_ref.1, bf16[512,128]{1,0:T(8,128)(2,1)} %b_ref.1), custom_call_target="tpu_custom_call" | custom-call | tf_op jit(solution)/shard_map/pallas_call | solution.py:302
  8.9 0.0 copy-start
  8.9 0.0 copy-start.1
  8.9 0.0 all-gather.5.cloned.1.call-update
  8.9 1.4 copy.10
  10.3 1.0 copy.11
  11.4 10.4 %all-to-all-start = ((bf16[16,128,128]{2,1,0:T(8,128)(2,1)}), bf16[16,128,128]{2,1,0:T(8,128)(2,1)S(1)}, u32[]{:S(2)}, u32[]{:S(2)}) async-start(bf16[16,128,128]{2,1,0:T(8,128)(2,1)} %bitcast.6), calls=%async_computation | async-start | bytes 1048576 | tf_op jit(solution)/shard_map/all_to_all | solution.py:311
  21.8 0.0 all-gather.7.cloned.1.call-start
  21.8 0.1 slice.3
  21.9 0.1 pad_maximum_fusion
  22.0 0.9 copy.13.next_ref
  22.9 0.9 copy.12.dt_ref
  23.8 15.6 %all-to-all-done.col_ref = bf16[16,128,128]{2,1,0:T(8,128)(2,1)S(1)} async-done(((bf16[16,128,128]{2,1,0:T(8,128)(2,1)}), bf16[16,128,128]{2,1,0:T(8,128)(2,1)S(1)}, u32[]{:S(2)}, u32[]{:S(2)}) %all-to-all-start) | async-done | bytes 524320 | tf_op jit(solution)/shard_map/all_to_all | solution.py:311
  39.3 0.9 copy-done.3
  40.3 1.0 copy-done.4
  41.2 1.4 shard_map.94
  42.6 21.7 %all-gather.5.cloned.1.call-done = bf16[16384,128]{1,0:T(8,128)(2,1)} async-done(((bf16[1024,128]{1,0:T(8,128)(2,1)}), bf16[16384,128]{1,0:T(8,128)(2,1)}) %all-gather.5.cloned.1.call-update) | async-done | bytes 4194320 | tf_op jit(solution)/shard_map/all_gather | solution.py:310
  64.3 3.9 %shard_map.95 = (f32[512,128]{1,0:T(8,128)S(1)}, f32[512,128]{1,0:T(8,128)S(1)}, f32[32,8,128]{2,1,0:T(8,128)S(1)}) custom-call(s32[1]{0:T(128)} %bitcast.me_ref, bf16[16,1024,128]{2,1,0:T(8,128)(2,1)} %bitcast.19, bf16[128,2048]{1,0:T(8,128)(2,1)S(1)} %copy-done, bf16[2048,128]{1,0:T(8,128)(2,1)S(1)} %copy-done.1, ...), custom_call_target="tpu_custom_call" | custom-call | flops 536870912 | bytes 7340032 | tf_op jit(solution)/shard_map/pallas_call | solution.py:324
  68.3 19.8 %all_to_all.30.carry_ref = f32[32,8,128]{2,1,0:T(8,128)S(1)} all-to-all(f32[32,8,128]{2,1,0:T(8,128)S(1)} %get-tuple-element.20), channel_id=1, replica_groups=mesh['seq'=32,'state'=16] {'seq'}, dimensions={0} | all-to-all | bytes 262144 | tf_op jit(solution)/shard_map/all_to_all | solution.py:297
  88.0 3.0 %shard_map.96 = (bf16[512,128]{1,0:T(8,128)(2,1)}, bf16[32,128,128]{2,1,0:T(8,128)(2,1)S(1)}, f32[1,128]{1,0:T(1,128)}) custom-call(s32[1]{0:T(128)} %bitcast.me_ref, f32[32,8,128]{2,1,0:T(8,128)S(1)} %all_to_all.30.carry_ref, bf16[16,1024,128]{2,1,0:T(8,128)(2,1)} %bitcast.20, f32[512,128]{1,0:T(8,128)S(1)} %get-tuple-element.21.st_ref, ...), custom_call_target="tpu_custom_call" | custom-call | flops 536870912 | bytes 7340032 | tf_op jit(solution)/shard_map/pallas_call | solution.py:334
  91.1 0.0 all-gather.7.cloned.1.call-update
  91.1 16.3 %all_to_all.31.parts_ref = bf16[4,1024,128]{2,1,0:T(8,128)(2,1)S(1)} all-to-all(bf16[4,1024,128]{2,1,0:T(8,128)(2,1)S(1)} %bitcast.17), channel_id=1, replica_groups={{0,128,256,384},{16,144,272,400},{32,160,288,416},{48,176,304,432},{64,..., dimensions={0} | all-to-all | bytes 2097152 | tf_op jit(solution)/shard_map/all_to_all | solution.py:297
  107.4 0.1 shard_map.98
  107.5 13.9 %all_to_all.32.parts_ref = bf16[8,128,128]{2,1,0:T(8,128)(2,1)S(1)} all-to-all(bf16[8,128,128]{2,1,0:T(8,128)(2,1)S(1)} %bitcast.15), channel_id=1, replica_groups={{0,16,32,48,64,80,96,112},{128,144,160,176,192,208,224,240},{256,272,28..., dimensions={0} | all-to-all | bytes 524288 | tf_op jit(solution)/shard_map/all_to_all | solution.py:297
  121.4 12.9 %all_to_all.33 = bf16[8,128,128]{2,1,0:T(8,128)(2,1)S(1)} all-to-all(bf16[8,128,128]{2,1,0:T(8,128)(2,1)S(1)} %shard_map.99), channel_id=1, replica_groups={{0,16,32,48,64,80,96,112},{128,144,160,176,192,208,224,240},{256,272,28..., dimensions={0} | all-to-all | bytes 524288 | tf_op jit(solution)/shard_map/all_to_all | solution.py:297
  134.3 1.1 shard_map.100
  135.4 4.9 %all-to-all-start.5 = ((bf16[4,1024,128]{2,1,0:T(8,128)(2,1)}), bf16[4,1024,128]{2,1,0:T(8,128)(2,1)S(1)}, u32[]{:S(2)}, u32[]{:S(2)}) async-start(bf16[4,1024,128]{2,1,0:T(8,128)(2,1)} %shard_map.100), calls=%async_computation.5 | async-start | bytes 2097152 | tf_op jit(solution)/shard_map/all_to_all | solution.py:297
  140.4 1.6 %copy-done.2 = bf16[8192,128]{1,0:T(8,128)(2,1)S(1)} copy-done((bf16[8192,128]{1,0:T(8,128)(2,1)S(1)}, bf16[8192,128]{1,0:T(8,128)(2,1)}, u32[]{:S(2)}) %copy-start.2) | copy-done | bytes 2097176
  142.0 1.4 shard_map.97
  143.3 7.2 %all-to-all-done.5 = bf16[4,1024,128]{2,1,0:T(8,128)(2,1)S(1)} async-done(((bf16[4,1024,128]{2,1,0:T(8,128)(2,1)}), bf16[4,1024,128]{2,1,0:T(8,128)(2,1)S(1)}, u32[]{:S(2)}, u32[]{:S(2)}) %all-to-all-start.5) | async-done | bytes 1048608 | tf_op jit(solution)/shard_map/all_to_all | solution.py:297
  150.5 1.5 shard_map.101
  (11 shorter events, 0.1 us)
Async XLA Ops:
  7.2 14.7 %copy-start.6 = (f32[512]{0:T(512)S(1)}, f32[512]{0:T(512)}, u32[]{:S(2)}) copy-start(f32[512]{0:T(512)} %param.11) | copy-start | bytes 6148
  7.2 57.2 %all-gather.5.cloned.1.call-start = ((), (), s32[]{:S(2)}) async-start(), calls=%async_computation.6 | async-start | bytes 4456448 | tf_op jit(solution)/shard_map/all_gather | solution.py:310
  8.9 30.4 %copy-start = (bf16[128,2048]{1,0:T(8,128)(2,1)S(1)}, bf16[128,2048]{1,0:T(8,128)(2,1)}, u32[]{:S(2)}) copy-start(bf16[128,2048]{1,0:T(8,128)(2,1)} %inp_ref.3) | copy-start | bytes 1572868
  8.9 30.4 %copy-start.1 = (bf16[2048,128]{1,0:T(8,128)(2,1)S(1)}, bf16[2048,128]{1,0:T(8,128)(2,1)}, u32[]{:S(2)}) copy-start(bf16[2048,128]{1,0:T(8,128)(2,1)} %outp_ref.3) | copy-start | bytes 1572868
  8.9 30.4 %copy-start.5 = (f32[128]{0:T(128)S(1)}, f32[128]{0:T(128)}, u32[]{:S(2)}) copy-start(f32[128]{0:T(128)} %param.10) | copy-start | bytes 1540
  11.4 28.0 %all-to-all-start = ((bf16[16,128,128]{2,1,0:T(8,128)(2,1)}), bf16[16,128,128]{2,1,0:T(8,128)(2,1)S(1)}, u32[]{:S(2)}, u32[]{:S(2)}) async-start(bf16[16,128,128]{2,1,0:T(8,128)(2,1)} %bitcast.6), calls=%async_computation | async-start | bytes 1048576 | tf_op jit(solution)/shard_map/all_to_all | solution.py:311
  21.8 118.6 %all-gather.7.cloned.1.call-start = ((), (), s32[]{:S(2)}) async-start(), calls=%async_computation.7 | async-start | bytes 2228224 | tf_op jit(solution)/shard_map/all_gather | solution.py:346
  39.3 1.0 copy-start.3
  40.3 1.0 copy-start.4
  135.4 15.1 %all-to-all-start.5 = ((bf16[4,1024,128]{2,1,0:T(8,128)(2,1)}), bf16[4,1024,128]{2,1,0:T(8,128)(2,1)S(1)}, u32[]{:S(2)}, u32[]{:S(2)}) async-start(bf16[4,1024,128]{2,1,0:T(8,128)(2,1)} %shard_map.100), calls=%async_computation.5 | async-start | bytes 2097152 | tf_op jit(solution)/shard_map/all_to_all | solution.py:297
  140.4 1.6 %copy-start.2 = (bf16[8192,128]{1,0:T(8,128)(2,1)S(1)}, bf16[8192,128]{1,0:T(8,128)(2,1)}, u32[]{:S(2)}) copy-start(bf16[8192,128]{1,0:T(8,128)(2,1)} %all-gather.7.cloned.1.call-done) | copy-start | bytes 6291460
Sparse Core Ops, SparseCore 0:
  10.7 53.5 all-gather.4
  91.2 36.5 all-gather.6

commit v4 on v3

--- a/solution.py
+++ b/solution.py
@@ -267,7 +267,9 @@
     done_ref[...] = jnp.zeros_like(done_ref)
     blocks = half_ref.shape[0]
     a = jnp.concatenate([half_ref[k] for k in range(blocks)], axis=1)
-    w = jnp.concatenate([col_ref[k] for k in range(blocks)], axis=0)
+    w = jnp.concatenate(
+        [col_ref[y, k] for k in range(blocks) for y in range(col_ref.shape[0])], axis=0
+    )
     out_ref[...] = jnp.dot(a, w, preferred_element_type=F32).astype(BF16)
 
 
@@ -308,9 +310,12 @@
         limit=60 * 1024 * 1024,
     )(inputs, out_grad)
     gathered = lax.all_gather(together, "state", axis=0)
-    columns = lax.all_to_all(
-        jnp.moveaxis(in_proj.reshape(LANES, blocks, LANES), 1, 0), "state", 0, 0, tiled=True
-    )
+    rows = LANES // INNER
+    place = lax.rem(lax.axis_index("seq").astype(jnp.int32), jnp.int32(INNER))
+    columns = lax.dynamic_slice_in_dim(in_proj, place * rows, rows, 0)
+    columns = jnp.moveaxis(columns.reshape(rows, blocks, LANES), 1, 0)
+    columns = lax.all_to_all(columns, "state", 0, 0, tiled=True)
+    columns = exchange(jnp.broadcast_to(columns, (INNER, *columns.shape)), along_y)
     following = jnp.concatenate([time_step[1:], jnp.zeros((1,), F32)])
     decays, whole, ends = call(
         decays_kernel,

time: 159 us -> 156 us (0.981)
  blocking collectives: 62.8 us -> 80.4 us
  waiting for transfers between devices: 44.5 us -> 27 us
  starting transfers between devices: 15.4 us -> 12.1 us
    all_to_all x0 -> x1, blocking collectives: none -> 18.1 us  [on_device(): columns = lax.all_to_all(columns, 'state', 0, 0, tiled=True)]
    all_gather x1, waiting for transfers between devices: 21.7 us -> 3.75 us  [on_device(): gathered = lax.all_gather(together, 'state', axis=0)]
    all_to_all x1 -> x2, waiting for transfers between devices: 7.22 us -> 23.3 us  [exchange(): return lax.all_to_all(x, 'seq', 0, 0, tiled=True, axis_index_groups=groups)]
    all_to_all x1 -> x0, waiting for transfers between devices: 15.6 us -> none  [on_device(): lax.all_to_all(jnp.moveaxis(in_proj.reshape(LANES, blocks, LANES), 1, 0),...]
    all_to_all x1 -> x0, starting transfers between devices: 10.4 us -> none  [on_device(): lax.all_to_all(jnp.moveaxis(in_proj.reshape(LANES, blocks, LANES), 1, 0),...]
    all_to_all x1 -> x2, starting transfers between devices: 4.94 us -> 12 us  [exchange(): return lax.all_to_all(x, 'seq', 0, 0, tiled=True, axis_index_groups=groups)]
    unnamed x15 -> x16, local copies, waits for them, and re-layouts: 4.9 us -> 4.37 us
  transfers between devices with their start and end apart: 4 -> 4, of which waited for: 3 -> 3; matrix products, arithmetic and copies ran while one was open for 3% -> 2% of each run, Pallas kernels for 3% -> 3%
where the time goes in v4:
time: 156 us; the launch traced here: 155 us
  blocking collectives  80.4 us (52%)
  waiting for transfers between devices  27 us (17%)
  Pallas kernels  14.2 us (9%)
  between operations  14.2 us (9%)
  starting transfers between devices  12.1 us (8%)
  local copies, waits for them, and re-layouts  7.08 us (5%)
    all_to_all x4, blocking collectives, exchange(): return lax.all_to_all(x, 'seq', 0, 0, tiled=True, axis_index_groups=groups)  62.3 us
    all_to_all x2, waiting for transfers between devices, exchange(): return lax.all_to_all(x, 'seq', 0, 0, tiled=True, axis_index_groups=groups)  23.3 us
    all_to_all x1, blocking collectives, on_device(): columns = lax.all_to_all(columns, 'state', 0, 0, tiled=True)  18.1 us
    all_to_all x2, starting transfers between devices, exchange(): return lax.all_to_all(x, 'seq', 0, 0, tiled=True, axis_index_groups=groups)  12 us
    unnamed x16, local copies, waits for them, and re-layouts  4.37 us
    pallas_call x1, Pallas kernels, on_device(): call(scans_kernel, (seen, seen, sds((devices, ROWS, LANES), F32)), in_spe...  3.91 us
    all_gather x1, waiting for transfers between devices, on_device(): gathered = lax.all_gather(together, 'state', axis=0)  3.75 us
  transfers between devices with their start and end apart: 4, of which 3 were waited for; matrix products, arithmetic and copies ran while one was open for 2% of the time, Pallas kernels for 3%

profile of v4, /device:TPU:2, one launch (start us, length us, event | category | flops | bytes accessed | tf_op | source)
XLA Modules:
  0.0 155.1 jit_solution(15274484975137343407)
XLA Ops:
  7.2 0.0 copy-start
  7.2 0.0 all-gather.5.cloned.1.call-start
  7.3 1.7 %shard_map.93 = bf16[1024,128]{1,0:T(8,128)(2,1)} custom-call(bf16[512,128]{1,0:T(8,128)(2,1)} %a_ref.1, bf16[512,128]{1,0:T(8,128)(2,1)} %b_ref.1), custom_call_target="tpu_custom_call" | custom-call | tf_op jit(solution)/shard_map/pallas_call | solution.py:304
  9.0 0.0 all-gather.5.cloned.1.call-update
  9.0 0.8 dynamic-slice_bitcast_fusion
  9.9 18.1 %all_to_all.35 = bf16[16,16,128]{2,1,0:T(8,128)(2,1)S(1)} all-to-all(bf16[16,16,128]{2,1,0:T(8,128)(2,1)S(1)} %copy.13), channel_id=1, replica_groups=mesh['seq'=32,'state'=16] {'state'}, dimensions={0} | all-to-all | bytes 131072 | tf_op jit(solution)/shard_map/all_to_all | solution.py:317
  28.0 0.9 broadcast_in_dim.15
  28.9 7.1 %all-to-all-start.1 = ((bf16[8,16,16,128]{3,2,1,0:T(8,128)(2,1)}), bf16[8,16,16,128]{3,2,1,0:T(8,128)(2,1)S(1)}, u32[]{:S(2)}, u32[]{:S(2)}) async-start(bf16[8,16,16,128]{3,2,1,0:T(8,128)(2,1)} %broadcast_in_dim.15), calls=%async_computation.1 | async-start | bytes 1048576 | tf_op jit(solution)/shard_map/all_to_all | solution.py:299
  36.0 0.0 all-gather.7.cloned.1.call-start
  36.0 0.1 slice.3
  36.1 0.1 pad_maximum_fusion
  36.2 0.9 copy.15.next_ref
  37.1 0.9 copy.14.dt_ref
  37.9 16.0 %all-to-all-done.1.col_ref = bf16[8,16,16,128]{3,2,1,0:T(8,128)(2,1)S(1)} async-done(((bf16[8,16,16,128]{3,2,1,0:T(8,128)(2,1)}), bf16[8,16,16,128]{3,2,1,0:T(8,128)(2,1)S(1)}, u32[]{:S(2)}, u32[]{:S(2)}) %all-to-all-start.1) | async-done | bytes 524320 | tf_op jit(solution)/shard_map/all_to_all | solution.py:299
  54.0 0.9 copy-done.3
  54.9 1.0 copy-done.4
  55.9 1.4 shard_map.94
  57.3 3.7 %all-gather.5.cloned.1.call-done = bf16[16384,128]{1,0:T(8,128)(2,1)} async-done(((bf16[1024,128]{1,0:T(8,128)(2,1)}), bf16[16384,128]{1,0:T(8,128)(2,1)}) %all-gather.5.cloned.1.call-update) | async-done | bytes 4194320 | tf_op jit(solution)/shard_map/all_gather | solution.py:312
  61.0 3.9 %shard_map.95 = (f32[512,128]{1,0:T(8,128)S(1)}, f32[512,128]{1,0:T(8,128)S(1)}, f32[32,8,128]{2,1,0:T(8,128)S(1)}) custom-call(s32[1]{0:T(128)} %bitcast.me_ref, bf16[16,1024,128]{2,1,0:T(8,128)(2,1)} %bitcast.22, bf16[128,2048]{1,0:T(8,128)(2,1)S(1)} %copy-done, bf16[2048,128]{1,0:T(8,128)(2,1)S(1)} %copy-done.1, ...), custom_call_target="tpu_custom_call" | custom-call | flops 536870912 | bytes 7340032 | tf_op jit(solution)/shard_map/pallas_call | solution.py:329
  65.0 19.3 %all_to_all.36.carry_ref = f32[32,8,128]{2,1,0:T(8,128)S(1)} all-to-all(f32[32,8,128]{2,1,0:T(8,128)S(1)} %get-tuple-element.20), channel_id=1, replica_groups=mesh['seq'=32,'state'=16] {'seq'}, dimensions={0} | all-to-all | bytes 262144 | tf_op jit(solution)/shard_map/all_to_all | solution.py:299
  84.2 3.0 %shard_map.96 = (bf16[512,128]{1,0:T(8,128)(2,1)}, bf16[32,128,128]{2,1,0:T(8,128)(2,1)S(1)}, f32[1,128]{1,0:T(1,128)}) custom-call(s32[1]{0:T(128)} %bitcast.me_ref, f32[32,8,128]{2,1,0:T(8,128)S(1)} %all_to_all.36.carry_ref, bf16[16,1024,128]{2,1,0:T(8,128)(2,1)} %bitcast.23, f32[512,128]{1,0:T(8,128)S(1)} %get-tuple-element.21.st_ref, ...), custom_call_target="tpu_custom_call" | custom-call | flops 536870912 | bytes 7340032 | tf_op jit(solution)/shard_map/pallas_call | solution.py:339
  87.3 0.0 all-gather.7.cloned.1.call-update
  87.3 16.3 %all_to_all.37.parts_ref = bf16[4,1024,128]{2,1,0:T(8,128)(2,1)S(1)} all-to-all(bf16[4,1024,128]{2,1,0:T(8,128)(2,1)S(1)} %bitcast.20), channel_id=1, replica_groups={{0,128,256,384},{16,144,272,400},{32,160,288,416},{48,176,304,432},{64,..., dimensions={0} | all-to-all | bytes 2097152 | tf_op jit(solution)/shard_map/all_to_all | solution.py:299
  103.6 0.1 shard_map.98
  103.7 13.9 %all_to_all.38.parts_ref = bf16[8,128,128]{2,1,0:T(8,128)(2,1)S(1)} all-to-all(bf16[8,128,128]{2,1,0:T(8,128)(2,1)S(1)} %bitcast.18), channel_id=1, replica_groups={{0,16,32,48,64,80,96,112},{128,144,160,176,192,208,224,240},{256,272,28..., dimensions={0} | all-to-all | bytes 524288 | tf_op jit(solution)/shard_map/all_to_all | solution.py:299
  117.6 12.9 %all_to_all.39 = bf16[8,128,128]{2,1,0:T(8,128)(2,1)S(1)} all-to-all(bf16[8,128,128]{2,1,0:T(8,128)(2,1)S(1)} %shard_map.99), channel_id=1, replica_groups={{0,16,32,48,64,80,96,112},{128,144,160,176,192,208,224,240},{256,272,28..., dimensions={0} | all-to-all | bytes 524288 | tf_op jit(solution)/shard_map/all_to_all | solution.py:299
  130.5 1.1 shard_map.100
  131.6 4.9 %all-to-all-start.6 = ((bf16[4,1024,128]{2,1,0:T(8,128)(2,1)}), bf16[4,1024,128]{2,1,0:T(8,128)(2,1)S(1)}, u32[]{:S(2)}, u32[]{:S(2)}) async-start(bf16[4,1024,128]{2,1,0:T(8,128)(2,1)} %shard_map.100), calls=%async_computation.6 | async-start | bytes 2097152 | tf_op jit(solution)/shard_map/all_to_all | solution.py:299
  136.6 1.6 %copy-done.2 = bf16[8192,128]{1,0:T(8,128)(2,1)S(1)} copy-done((bf16[8192,128]{1,0:T(8,128)(2,1)S(1)}, bf16[8192,128]{1,0:T(8,128)(2,1)}, u32[]{:S(2)}) %copy-start.2) | copy-done | bytes 2097176
  138.2 1.4 shard_map.97
  139.5 7.2 %all-to-all-done.6 = bf16[4,1024,128]{2,1,0:T(8,128)(2,1)S(1)} async-done(((bf16[4,1024,128]{2,1,0:T(8,128)(2,1)}), bf16[4,1024,128]{2,1,0:T(8,128)(2,1)S(1)}, u32[]{:S(2)}, u32[]{:S(2)}) %all-to-all-start.6) | async-done | bytes 1048608 | tf_op jit(solution)/shard_map/all_to_all | solution.py:299
  146.7 1.5 shard_map.101
  (14 shorter events, 0.1 us)
Async XLA Ops:
  7.2 46.8 %copy-start = (bf16[128,2048]{1,0:T(8,128)(2,1)S(1)}, bf16[128,2048]{1,0:T(8,128)(2,1)}, u32[]{:S(2)}) copy-start(bf16[128,2048]{1,0:T(8,128)(2,1)} %inp_ref.3) | copy-start | bytes 1572868
  7.2 28.8 %copy-start.6 = (f32[512]{0:T(512)S(1)}, f32[512]{0:T(512)}, u32[]{:S(2)}) copy-start(f32[512]{0:T(512)} %param.11) | copy-start | bytes 6148
  7.2 46.8 %copy-start.1 = (bf16[2048,128]{1,0:T(8,128)(2,1)S(1)}, bf16[2048,128]{1,0:T(8,128)(2,1)}, u32[]{:S(2)}) copy-start(bf16[2048,128]{1,0:T(8,128)(2,1)} %outp_ref.3) | copy-start | bytes 1572868
  7.2 46.8 %copy-start.5 = (f32[128]{0:T(128)S(1)}, f32[128]{0:T(128)}, u32[]{:S(2)}) copy-start(f32[128]{0:T(128)} %param.10) | copy-start | bytes 1540
  7.2 53.8 %all-gather.5.cloned.1.call-start = ((), (), s32[]{:S(2)}) async-start(), calls=%async_computation.7 | async-start | bytes 4456448 | tf_op jit(solution)/shard_map/all_gather | solution.py:312
  28.9 25.1 %all-to-all-start.1 = ((bf16[8,16,16,128]{3,2,1,0:T(8,128)(2,1)}), bf16[8,16,16,128]{3,2,1,0:T(8,128)(2,1)S(1)}, u32[]{:S(2)}, u32[]{:S(2)}) async-start(bf16[8,16,16,128]{3,2,1,0:T(8,128)(2,1)} %broadcast_in_dim.15), calls=%async_computation.1 | async-start | bytes 1048576 | tf_op jit(solution)/shard_map/all_to_all | solution.py:299
  36.0 100.6 %all-gather.7.cloned.1.call-start = ((), (), s32[]{:S(2)}) async-start(), calls=%async_computation.8 | async-start | bytes 2228224 | tf_op jit(solution)/shard_map/all_gather | solution.py:351
  54.0 1.0 copy-start.3
  54.9 1.0 copy-start.4
  131.6 15.1 %all-to-all-start.6 = ((bf16[4,1024,128]{2,1,0:T(8,128)(2,1)}), bf16[4,1024,128]{2,1,0:T(8,128)(2,1)S(1)}, u32[]{:S(2)}, u32[]{:S(2)}) async-start(bf16[4,1024,128]{2,1,0:T(8,128)(2,1)} %shard_map.100), calls=%async_computation.6 | async-start | bytes 2097152 | tf_op jit(solution)/shard_map/all_to_all | solution.py:299
  136.6 1.6 %copy-start.2 = (bf16[8192,128]{1,0:T(8,128)(2,1)S(1)}, bf16[8192,128]{1,0:T(8,128)(2,1)}, u32[]{:S(2)}) copy-start(bf16[8192,128]{1,0:T(8,128)(2,1)} %all-gather.7.cloned.1.call-done) | copy-start | bytes 6291460
Sparse Core Ops, SparseCore 0:
  10.7 50.2 all-gather.4
  87.4 36.1 all-gather.6

commit v5 on v4

--- a/solution.py
+++ b/solution.py
@@ -14,8 +14,8 @@
 VMEM = pl.BlockSpec(memory_space=pltpu.VMEM)
 SMEM = pl.BlockSpec(memory_space=pltpu.SMEM)
 HBM = pl.BlockSpec(memory_space=pltpu.HBM)
-SCANS = 48 * 1024 * 1024
-PRODS = 48 * 1024 * 1024
+SCANS = 46 * 1024 * 1024
+PRODS = 46 * 1024 * 1024
 ANY = pl.BlockSpec(memory_space=pl.ANY)
 DECAY, NEAR, FAR, NEXT, FIRST, KINDS = range(6)
 CUM, REM = range(2)
@@ -118,7 +118,7 @@
 
 def scans_kernel(
     me_ref, g_ref, inp_ref, outp_ref, d_ref, b_ref, ends_ref,
-    st_ref, ad_ref, carry_ref, drive, adj_in, held, sems,
+    st_ref, ad_ref, carry_ref, held, drive, adj_in, sems,
 ):
     copies, step = fetch_parts(g_ref, held, sems)
     tokens = st_ref.shape[0]
@@ -198,9 +198,8 @@
 
 def products_kernel(
     me_ref, carry_ref, g_ref, st_ref, ad_ref, b_ref,
-    half_ref, grads_ref, rates_ref, into, back, held, sems,
+    half_ref, grads_ref, rates_ref, into, back,
 ):
-    copies, step = fetch_parts(g_ref, held, sems)
     devices = carry_ref.shape[0]
     blocks, both, _ = g_ref.shape
     tokens = both // 2
@@ -226,10 +225,8 @@
     half_ref[...] = adjoint
     half = LANES // 2
     for k in range(0, blocks, 2):
-        if k % step == 0:
-            copies[k // step].wait()
-        x = jnp.concatenate([held[k, :tokens, :], held[k + 1, :tokens, :]], axis=1)
-        y = jnp.concatenate([held[k, tokens:, :], held[k + 1, tokens:, :]], axis=1)
+        x = jnp.concatenate([g_ref[k, :tokens, :], g_ref[k + 1, :tokens, :]], axis=1)
+        y = jnp.concatenate([g_ref[k, tokens:, :], g_ref[k + 1, tokens:, :]], axis=1)
         gi = lax.dot_general(adjoint, x, (((0,), (0,)), ((), ())), preferred_element_type=F32)
         go = lax.dot_general(state, y, (((0,), (0,)), ((), ())), preferred_element_type=F32)
         for q in range(2):
@@ -326,12 +323,11 @@
         ),
         in_specs=[VMEM] * 5 + [ANY],
     )(time_step[:, None], following[:, None], rates[None, :], in_proj, out_proj, columns)
-    states, adjoints, carry = call(
+    states, adjoints, carry, gathered = call(
         scans_kernel,
-        (seen, seen, sds((devices, ROWS, LANES), F32)),
+        (seen, seen, sds((devices, ROWS, LANES), F32), sds(gathered.shape, BF16)),
         in_specs=[SMEM, HBM] + [VMEM] * 5,
-        scratch=[pltpu.VMEM((tokens, LANES), F32)] * 2
-        + parted(gathered.shape),
+        scratch=[pltpu.VMEM((tokens, LANES), F32)] * 2 + [pltpu.SemaphoreType.DMA((PARTS,))],
         cost=estimate(4 * tokens * features * LANES, 7 << 20),
         limit=SCANS,
     )(me, gathered, in_proj, out_proj, decays, whole, ends)
@@ -343,8 +339,8 @@
             sds((devices, features * 2 // devices, LANES), BF16),
             sds((1, LANES), F32),
         ),
-        in_specs=[SMEM, VMEM, HBM, VMEM, VMEM, VMEM],
-        scratch=[pltpu.VMEM((devices, LANES), F32)] * 2 + parted(gathered.shape),
+        in_specs=[SMEM] + [VMEM] * 5,
+        scratch=[pltpu.VMEM((devices, LANES), F32)] * 2,
         cost=estimate(4 * tokens * features * LANES, 7 << 20),
         limit=PRODS,
     )(me, carry, gathered, states, adjoints, whole)

time: 156 us -> 154 us (0.987)
  local copies, waits for them, and re-layouts: 7.08 us -> 11.2 us
  waiting for transfers between devices: 27 us -> 23.1 us
  Pallas kernels: 14.2 us -> 12.5 us
    unnamed x16 -> x18, local copies, waits for them, and re-layouts: 4.37 us -> 7.12 us
    all_gather x1, waiting for transfers between devices: 3.75 us -> 1.16 us  [on_device(): gathered = lax.all_gather(together, 'state', axis=0)]
    pallas_call x1, Pallas kernels: 3.04 us -> 1.37 us  [on_device(): call(products_kernel, (sds((tokens, LANES), BF16), sds((devices, features...]
  transfers between devices with their start and end apart: 4 -> 4, of which waited for: 3 -> 3; matrix products, arithmetic and copies ran while one was open for 2% -> 3% of each run, Pallas kernels for 3% -> 3%
where the time goes in v5:
time: 154 us; the launch traced here: 153 us
  blocking collectives  80.3 us (52%)
  waiting for transfers between devices  23.1 us (15%)
  between operations  14.1 us (9%)
  Pallas kernels  12.5 us (8%)
  starting transfers between devices  12.1 us (8%)
  local copies, waits for them, and re-layouts  11.2 us (7%)
    all_to_all x4, blocking collectives, exchange(): return lax.all_to_all(x, 'seq', 0, 0, tiled=True, axis_index_groups=groups)  62.2 us
    all_to_all x2, waiting for transfers between devices, exchange(): return lax.all_to_all(x, 'seq', 0, 0, tiled=True, axis_index_groups=groups)  21.9 us
    all_to_all x1, blocking collectives, on_device(): columns = lax.all_to_all(columns, 'state', 0, 0, tiled=True)  18.1 us
    all_to_all x2, starting transfers between devices, exchange(): return lax.all_to_all(x, 'seq', 0, 0, tiled=True, axis_index_groups=groups)  12 us
    unnamed x18, local copies, waits for them, and re-layouts  7.12 us
    pallas_call x1, Pallas kernels, on_device(): call(scans_kernel, (seen, seen, sds((devices, ROWS, LANES), F32), sds(gat...  3.92 us
  transfers between devices with their start and end apart: 4, of which 3 were waited for; matrix products, arithmetic and copies ran while one was open for 3% of the time, Pallas kernels for 3%

profile of v5, /device:TPU:2, one launch (start us, length us, event | category | flops | bytes accessed | tf_op | source)
XLA Modules:
  0.0 153.4 jit_solution(16132919763677712034)
XLA Ops:
  7.2 0.0 all-gather.5.cloned.1.call-start
  7.2 1.7 %shard_map.93 = bf16[1024,128]{1,0:T(8,128)(2,1)} custom-call(bf16[512,128]{1,0:T(8,128)(2,1)} %a_ref.1, bf16[512,128]{1,0:T(8,128)(2,1)} %b_ref.1), custom_call_target="tpu_custom_call" | custom-call | tf_op jit(solution)/shard_map/pallas_call | solution.py:301
  9.0 0.8 dynamic-slice_bitcast_fusion
  9.9 18.1 %all_to_all.35 = bf16[16,16,128]{2,1,0:T(8,128)(2,1)S(1)} all-to-all(bf16[16,16,128]{2,1,0:T(8,128)(2,1)S(1)} %copy.13), channel_id=1, replica_groups=mesh['seq'=32,'state'=16] {'state'}, dimensions={0} | all-to-all | bytes 131072 | tf_op jit(solution)/shard_map/all_to_all | solution.py:314
  28.0 0.9 broadcast_in_dim.15
  28.9 7.1 %all-to-all-start.1 = ((bf16[8,16,16,128]{3,2,1,0:T(8,128)(2,1)}), bf16[8,16,16,128]{3,2,1,0:T(8,128)(2,1)S(1)}, u32[]{:S(2)}, u32[]{:S(2)}) async-start(bf16[8,16,16,128]{3,2,1,0:T(8,128)(2,1)} %broadcast_in_dim.15), calls=%async_computation.1 | async-start | bytes 1048576 | tf_op jit(solution)/shard_map/all_to_all | solution.py:296
  36.0 0.0 all-gather.7.cloned.1.call-start
  36.0 0.8 slice.3
  36.8 0.1 pad_maximum_fusion
  36.8 0.9 copy.15.next_ref
  37.7 1.6 %copy.14.dt_ref = f32[512,1]{1,0:T(8,128)} copy(f32[512,1]{0,1:T(1,128)} %bitcast.24) | data formatting | bytes 4096 | tf_op jit(solution)/shard_map/broadcast_in_dim | solution.py:325
  39.3 14.7 %all-to-all-done.1.col_ref = bf16[8,16,16,128]{3,2,1,0:T(8,128)(2,1)S(1)} async-done(((bf16[8,16,16,128]{3,2,1,0:T(8,128)(2,1)}), bf16[8,16,16,128]{3,2,1,0:T(8,128)(2,1)S(1)}, u32[]{:S(2)}, u32[]{:S(2)}) %all-to-all-start.1) | async-done | bytes 524320 | tf_op jit(solution)/shard_map/all_to_all | solution.py:296
  54.0 1.0 copy-done
  55.0 1.0 copy-done.2
  56.1 1.0 copy-done.5
  57.0 0.9 copy-done.6
  58.0 0.7 copy-done.7
  58.6 1.4 shard_map.94
  60.0 1.2 all-gather.5.cloned.1.call-done
  61.2 3.9 %shard_map.95 = (f32[512,128]{1,0:T(8,128)S(1)}, f32[512,128]{1,0:T(8,128)S(1)}, f32[32,8,128]{2,1,0:T(8,128)S(1)}, bf16[16,1024,128]{2,1,0:T(8,128)(2,1)S(1)}) custom-call(s32[1]{0:T(128)} %bitcast.me_ref, bf16[16,1024,128]{2,1,0:T(8,128)(2,1)} %bitcast.22, bf16[128,2048]{1,0:T(8,128)(2,1)S(1)} %copy-done.1, bf16[2048,128]{1,0:T(8,128)(2,1)S(1)} %copy-done.3, ...), custom_call_target="tpu_custom_call" | custom-call | flops 536870912 | bytes 7340032 | tf_op jit(solution)/shard_map/pallas_call | solution.py:326
  65.1 19.1 %all_to_all.36.carry_ref = f32[32,8,128]{2,1,0:T(8,128)S(1)} all-to-all(f32[32,8,128]{2,1,0:T(8,128)S(1)} %get-tuple-element.21), channel_id=1, replica_groups=mesh['seq'=32,'state'=16] {'seq'}, dimensions={0} | all-to-all | bytes 262144 | tf_op jit(solution)/shard_map/all_to_all | solution.py:296
  84.2 1.4 shard_map.96
  85.6 16.3 %all_to_all.37.parts_ref = bf16[4,1024,128]{2,1,0:T(8,128)(2,1)S(1)} all-to-all(bf16[4,1024,128]{2,1,0:T(8,128)(2,1)S(1)} %bitcast.20), channel_id=1, replica_groups={{0,128,256,384},{16,144,272,400},{32,160,288,416},{48,176,304,432},{64,..., dimensions={0} | all-to-all | bytes 2097152 | tf_op jit(solution)/shard_map/all_to_all | solution.py:296
  101.9 0.1 shard_map.98
  102.1 13.9 %all_to_all.38.parts_ref = bf16[8,128,128]{2,1,0:T(8,128)(2,1)S(1)} all-to-all(bf16[8,128,128]{2,1,0:T(8,128)(2,1)S(1)} %bitcast.18), channel_id=1, replica_groups={{0,16,32,48,64,80,96,112},{128,144,160,176,192,208,224,240},{256,272,28..., dimensions={0} | all-to-all | bytes 524288 | tf_op jit(solution)/shard_map/all_to_all | solution.py:296
  116.0 12.9 %all_to_all.39 = bf16[8,128,128]{2,1,0:T(8,128)(2,1)S(1)} all-to-all(bf16[8,128,128]{2,1,0:T(8,128)(2,1)S(1)} %shard_map.99), channel_id=1, replica_groups={{0,16,32,48,64,80,96,112},{128,144,160,176,192,208,224,240},{256,272,28..., dimensions={0} | all-to-all | bytes 524288 | tf_op jit(solution)/shard_map/all_to_all | solution.py:296
  128.9 1.1 shard_map.100
  129.9 4.9 %all-to-all-start.6 = ((bf16[4,1024,128]{2,1,0:T(8,128)(2,1)}), bf16[4,1024,128]{2,1,0:T(8,128)(2,1)S(1)}, u32[]{:S(2)}, u32[]{:S(2)}) async-start(bf16[4,1024,128]{2,1,0:T(8,128)(2,1)} %shard_map.100), calls=%async_computation.6 | async-start | bytes 2097152 | tf_op jit(solution)/shard_map/all_to_all | solution.py:296
  134.9 1.6 %copy-done.4 = bf16[8192,128]{1,0:T(8,128)(2,1)S(1)} copy-done((bf16[8192,128]{1,0:T(8,128)(2,1)S(1)}, bf16[8192,128]{1,0:T(8,128)(2,1)}, u32[]{:S(2)}) %copy-start.4) | copy-done | bytes 2097176
  136.5 1.4 shard_map.97
  137.9 7.2 %all-to-all-done.6 = bf16[4,1024,128]{2,1,0:T(8,128)(2,1)S(1)} async-done(((bf16[4,1024,128]{2,1,0:T(8,128)(2,1)}), bf16[4,1024,128]{2,1,0:T(8,128)(2,1)S(1)}, u32[]{:S(2)}, u32[]{:S(2)}) %all-to-all-start.6) | async-done | bytes 1048608 | tf_op jit(solution)/shard_map/all_to_all | solution.py:296
  145.1 1.5 shard_map.101
  (16 shorter events, 0.1 us)
Async XLA Ops:
  7.2 54.0 %copy-start.1 = (bf16[128,2048]{1,0:T(8,128)(2,1)S(1)}, bf16[128,2048]{1,0:T(8,128)(2,1)}, u32[]{:S(2)}) copy-start(bf16[128,2048]{1,0:T(8,128)(2,1)} %inp_ref.3) | copy-start | bytes 1572868
  7.2 54.0 %copy-start.3 = (bf16[2048,128]{1,0:T(8,128)(2,1)S(1)}, bf16[2048,128]{1,0:T(8,128)(2,1)}, u32[]{:S(2)}) copy-start(bf16[2048,128]{1,0:T(8,128)(2,1)} %outp_ref.3) | copy-start | bytes 1572868
  7.2 54.0 %all-gather.5.cloned.1.call-start = ((), (), s32[]{:S(2)}) async-start(), calls=%async_computation.7 | async-start | bytes 4456448 | tf_op jit(solution)/shard_map/all_gather | solution.py:309
  28.9 25.1 %all-to-all-start.1 = ((bf16[8,16,16,128]{3,2,1,0:T(8,128)(2,1)}), bf16[8,16,16,128]{3,2,1,0:T(8,128)(2,1)S(1)}, u32[]{:S(2)}, u32[]{:S(2)}) async-start(bf16[8,16,16,128]{3,2,1,0:T(8,128)(2,1)} %broadcast_in_dim.15), calls=%async_computation.1 | async-start | bytes 1048576 | tf_op jit(solution)/shard_map/all_to_all | solution.py:296
  36.0 98.9 %all-gather.7.cloned.1.call-start = ((), (), s32[]{:S(2)}) async-start(), calls=%async_computation.8 | async-start | bytes 2228224 | tf_op jit(solution)/shard_map/all_gather | solution.py:347
  54.0 1.0 copy-start
  55.0 1.1 copy-start.2
  56.1 1.0 copy-start.5
  57.0 0.9 copy-start.6
  58.0 0.7 copy-start.7
  129.9 15.1 %all-to-all-start.6 = ((bf16[4,1024,128]{2,1,0:T(8,128)(2,1)}), bf16[4,1024,128]{2,1,0:T(8,128)(2,1)S(1)}, u32[]{:S(2)}, u32[]{:S(2)}) async-start(bf16[4,1024,128]{2,1,0:T(8,128)(2,1)} %shard_map.100), calls=%async_computation.6 | async-start | bytes 2097152 | tf_op jit(solution)/shard_map/all_to_all | solution.py:296
  134.9 1.6 %copy-start.4 = (bf16[8192,128]{1,0:T(8,128)(2,1)S(1)}, bf16[8192,128]{1,0:T(8,128)(2,1)}, u32[]{:S(2)}) copy-start(bf16[8192,128]{1,0:T(8,128)(2,1)} %all-gather.7.cloned.1.call-done) | copy-start | bytes 6291460
Sparse Core Ops, SparseCore 0:
  10.7 50.4 all-gather.4
  85.7 36.2 all-gather.6

commit v6 on v5

--- a/solution.py
+++ b/solution.py
@@ -80,7 +80,7 @@
     )
 
 
-PARTS = 4
+PARTS = 8
 
 
 def join_kernel(a_ref, b_ref, out_ref, held, sems):

time: 154 us -> 154 us (level)
  no operation moved by 1% of the time
where the time goes in v6:
time: 154 us; the launch traced here: 153 us
  blocking collectives  80.3 us (52%)
  waiting for transfers between devices  23.1 us (15%)
  between operations  14.1 us (9%)
  Pallas kernels  12.4 us (8%)
  starting transfers between devices  12.1 us (8%)
  local copies, waits for them, and re-layouts  11.2 us (7%)
    all_to_all x4, blocking collectives, exchange(): return lax.all_to_all(x, 'seq', 0, 0, tiled=True, axis_index_groups=groups)  62.2 us
    all_to_all x2, waiting for transfers between devices, exchange(): return lax.all_to_all(x, 'seq', 0, 0, tiled=True, axis_index_groups=groups)  21.9 us
    all_to_all x1, blocking collectives, on_device(): columns = lax.all_to_all(columns, 'state', 0, 0, tiled=True)  18.1 us
    all_to_all x2, starting transfers between devices, exchange(): return lax.all_to_all(x, 'seq', 0, 0, tiled=True, axis_index_groups=groups)  12 us
    unnamed x18, local copies, waits for them, and re-layouts  7.12 us
    pallas_call x1, Pallas kernels, on_device(): call(scans_kernel, (seen, seen, sds((devices, ROWS, LANES), F32), sds(gat...  3.81 us
  transfers between devices with their start and end apart: 4, of which 3 were waited for; matrix products, arithmetic and copies ran while one was open for 3% of the time, Pallas kernels for 3%

profile of v6, /device:TPU:2, one launch (start us, length us, event | category | flops | bytes accessed | tf_op | source)
XLA Modules:
  0.0 153.3 jit_solution(3437759073003173461)
XLA Ops:
  7.2 0.0 all-gather.5.cloned.1.call-start
  7.2 1.7 %shard_map.93 = bf16[1024,128]{1,0:T(8,128)(2,1)} custom-call(bf16[512,128]{1,0:T(8,128)(2,1)} %a_ref.1, bf16[512,128]{1,0:T(8,128)(2,1)} %b_ref.1), custom_call_target="tpu_custom_call" | custom-call | tf_op jit(solution)/shard_map/pallas_call | solution.py:301
  9.0 0.8 dynamic-slice_bitcast_fusion
  9.9 18.1 %all_to_all.35 = bf16[16,16,128]{2,1,0:T(8,128)(2,1)S(1)} all-to-all(bf16[16,16,128]{2,1,0:T(8,128)(2,1)S(1)} %copy.13), channel_id=1, replica_groups=mesh['seq'=32,'state'=16] {'state'}, dimensions={0} | all-to-all | bytes 131072 | tf_op jit(solution)/shard_map/all_to_all | solution.py:314
  28.0 0.9 broadcast_in_dim.15
  28.9 7.1 %all-to-all-start.1 = ((bf16[8,16,16,128]{3,2,1,0:T(8,128)(2,1)}), bf16[8,16,16,128]{3,2,1,0:T(8,128)(2,1)S(1)}, u32[]{:S(2)}, u32[]{:S(2)}) async-start(bf16[8,16,16,128]{3,2,1,0:T(8,128)(2,1)} %broadcast_in_dim.15), calls=%async_computation.1 | async-start | bytes 1048576 | tf_op jit(solution)/shard_map/all_to_all | solution.py:296
  36.0 0.0 all-gather.7.cloned.1.call-start
  36.0 0.8 slice.3
  36.8 0.1 pad_maximum_fusion
  36.8 0.9 copy.15.next_ref
  37.7 1.6 %copy.14.dt_ref = f32[512,1]{1,0:T(8,128)} copy(f32[512,1]{0,1:T(1,128)} %bitcast.24) | data formatting | bytes 4096 | tf_op jit(solution)/shard_map/broadcast_in_dim | solution.py:325
  39.3 14.7 %all-to-all-done.1.col_ref = bf16[8,16,16,128]{3,2,1,0:T(8,128)(2,1)S(1)} async-done(((bf16[8,16,16,128]{3,2,1,0:T(8,128)(2,1)}), bf16[8,16,16,128]{3,2,1,0:T(8,128)(2,1)S(1)}, u32[]{:S(2)}, u32[]{:S(2)}) %all-to-all-start.1) | async-done | bytes 524320 | tf_op jit(solution)/shard_map/all_to_all | solution.py:296
  54.0 1.0 copy-done
  55.0 1.0 copy-done.2
  56.1 1.0 copy-done.5
  57.0 0.9 copy-done.6
  58.0 0.7 copy-done.7
  58.6 1.4 shard_map.94
  60.0 1.2 all-gather.5.cloned.1.call-done
  61.2 3.8 %shard_map.95 = (f32[512,128]{1,0:T(8,128)S(1)}, f32[512,128]{1,0:T(8,128)S(1)}, f32[32,8,128]{2,1,0:T(8,128)S(1)}, bf16[16,1024,128]{2,1,0:T(8,128)(2,1)S(1)}) custom-call(s32[1]{0:T(128)} %bitcast.me_ref, bf16[16,1024,128]{2,1,0:T(8,128)(2,1)} %bitcast.22, bf16[128,2048]{1,0:T(8,128)(2,1)S(1)} %copy-done.1, bf16[2048,128]{1,0:T(8,128)(2,1)S(1)} %copy-done.3, ...), custom_call_target="tpu_custom_call" | custom-call | flops 536870912 | bytes 7340032 | tf_op jit(solution)/shard_map/pallas_call | solution.py:326
  65.0 19.1 %all_to_all.36.carry_ref = f32[32,8,128]{2,1,0:T(8,128)S(1)} all-to-all(f32[32,8,128]{2,1,0:T(8,128)S(1)} %get-tuple-element.21), channel_id=1, replica_groups=mesh['seq'=32,'state'=16] {'seq'}, dimensions={0} | all-to-all | bytes 262144 | tf_op jit(solution)/shard_map/all_to_all | solution.py:296
  84.1 1.4 shard_map.96
  85.5 16.3 %all_to_all.37.parts_ref = bf16[4,1024,128]{2,1,0:T(8,128)(2,1)S(1)} all-to-all(bf16[4,1024,128]{2,1,0:T(8,128)(2,1)S(1)} %bitcast.20), channel_id=1, replica_groups={{0,128,256,384},{16,144,272,400},{32,160,288,416},{48,176,304,432},{64,..., dimensions={0} | all-to-all | bytes 2097152 | tf_op jit(solution)/shard_map/all_to_all | solution.py:296
  101.8 0.1 shard_map.98
  101.9 13.9 %all_to_all.38.parts_ref = bf16[8,128,128]{2,1,0:T(8,128)(2,1)S(1)} all-to-all(bf16[8,128,128]{2,1,0:T(8,128)(2,1)S(1)} %bitcast.18), channel_id=1, replica_groups={{0,16,32,48,64,80,96,112},{128,144,160,176,192,208,224,240},{256,272,28..., dimensions={0} | all-to-all | bytes 524288 | tf_op jit(solution)/shard_map/all_to_all | solution.py:296
  115.8 12.9 %all_to_all.39 = bf16[8,128,128]{2,1,0:T(8,128)(2,1)S(1)} all-to-all(bf16[8,128,128]{2,1,0:T(8,128)(2,1)S(1)} %shard_map.99), channel_id=1, replica_groups={{0,16,32,48,64,80,96,112},{128,144,160,176,192,208,224,240},{256,272,28..., dimensions={0} | all-to-all | bytes 524288 | tf_op jit(solution)/shard_map/all_to_all | solution.py:296
  128.7 1.1 shard_map.100
  129.8 4.9 %all-to-all-start.6 = ((bf16[4,1024,128]{2,1,0:T(8,128)(2,1)}), bf16[4,1024,128]{2,1,0:T(8,128)(2,1)S(1)}, u32[]{:S(2)}, u32[]{:S(2)}) async-start(bf16[4,1024,128]{2,1,0:T(8,128)(2,1)} %shard_map.100), calls=%async_computation.6 | async-start | bytes 2097152 | tf_op jit(solution)/shard_map/all_to_all | solution.py:296
  134.8 1.6 %copy-done.4 = bf16[8192,128]{1,0:T(8,128)(2,1)S(1)} copy-done((bf16[8192,128]{1,0:T(8,128)(2,1)S(1)}, bf16[8192,128]{1,0:T(8,128)(2,1)}, u32[]{:S(2)}) %copy-start.4) | copy-done | bytes 2097176
  136.4 1.4 shard_map.97
  137.7 7.2 %all-to-all-done.6 = bf16[4,1024,128]{2,1,0:T(8,128)(2,1)S(1)} async-done(((bf16[4,1024,128]{2,1,0:T(8,128)(2,1)}), bf16[4,1024,128]{2,1,0:T(8,128)(2,1)S(1)}, u32[]{:S(2)}, u32[]{:S(2)}) %all-to-all-start.6) | async-done | bytes 1048608 | tf_op jit(solution)/shard_map/all_to_all | solution.py:296
  144.9 1.5 shard_map.101
  (16 shorter events, 0.1 us)
Async XLA Ops:
  7.2 54.0 %copy-start.1 = (bf16[128,2048]{1,0:T(8,128)(2,1)S(1)}, bf16[128,2048]{1,0:T(8,128)(2,1)}, u32[]{:S(2)}) copy-start(bf16[128,2048]{1,0:T(8,128)(2,1)} %inp_ref.3) | copy-start | bytes 1572868
  7.2 54.0 %copy-start.3 = (bf16[2048,128]{1,0:T(8,128)(2,1)S(1)}, bf16[2048,128]{1,0:T(8,128)(2,1)}, u32[]{:S(2)}) copy-start(bf16[2048,128]{1,0:T(8,128)(2,1)} %outp_ref.3) | copy-start | bytes 1572868
  7.2 54.0 %all-gather.5.cloned.1.call-start = ((), (), s32[]{:S(2)}) async-start(), calls=%async_computation.7 | async-start | bytes 4456448 | tf_op jit(solution)/shard_map/all_gather | solution.py:309
  28.9 25.1 %all-to-all-start.1 = ((bf16[8,16,16,128]{3,2,1,0:T(8,128)(2,1)}), bf16[8,16,16,128]{3,2,1,0:T(8,128)(2,1)S(1)}, u32[]{:S(2)}, u32[]{:S(2)}) async-start(bf16[8,16,16,128]{3,2,1,0:T(8,128)(2,1)} %broadcast_in_dim.15), calls=%async_computation.1 | async-start | bytes 1048576 | tf_op jit(solution)/shard_map/all_to_all | solution.py:296
  36.0 98.8 %all-gather.7.cloned.1.call-start = ((), (), s32[]{:S(2)}) async-start(), calls=%async_computation.8 | async-start | bytes 2228224 | tf_op jit(solution)/shard_map/all_gather | solution.py:347
  54.0 1.0 copy-start
  55.0 1.1 copy-start.2
  56.1 1.0 copy-start.5
  57.0 0.9 copy-start.6
  58.0 0.7 copy-start.7
  129.8 15.1 %all-to-all-start.6 = ((bf16[4,1024,128]{2,1,0:T(8,128)(2,1)}), bf16[4,1024,128]{2,1,0:T(8,128)(2,1)S(1)}, u32[]{:S(2)}, u32[]{:S(2)}) async-start(bf16[4,1024,128]{2,1,0:T(8,128)(2,1)} %shard_map.100), calls=%async_computation.6 | async-start | bytes 2097152 | tf_op jit(solution)/shard_map/all_to_all | solution.py:296
  134.8 1.6 %copy-start.4 = (bf16[8192,128]{1,0:T(8,128)(2,1)S(1)}, bf16[8192,128]{1,0:T(8,128)(2,1)}, u32[]{:S(2)}) copy-start(bf16[8192,128]{1,0:T(8,128)(2,1)} %all-gather.7.cloned.1.call-done) | copy-start | bytes 6291460
Sparse Core Ops, SparseCore 0:
  10.7 50.4 all-gather.4
  85.6 36.2 all-gather.6
